TPU v7x, 32 devices: a whole 2x2x4 slice. The times are simulated.
32 devices in a mesh: slab: 4 (over y, x), plane: 8 (over z, core).
Axes of the slice: x: 2, y: 2, z: 4, core: 2. Of those that a mesh axis runs over, the one named last changes fastest.
Arguments:
- images: float32 [2, 32, 128, 1024], P(None, 'slab', 'plane'), may hold values from -12 to 12, as said below
- shifts: int32 [3, 4, 16, 128], P(None, 'slab', 'plane'), may hold values from -1 to 1
- initial_displacement: float32 [3, 4, 16, 128], P(None, 'slab', 'plane'), may hold values from -2 to 2
Outputs:
- displacement: float32 [3, 4, 16, 128], P(None, 'slab', 'plane')
- mismatch: float32 [32, 128, 1024], P('slab', 'plane')
Inputs may be any that keep to these rules, and one draw needn't show every extreme that they name: `images`: voxel intensities.
All inputs are finite; a program needn't handle non-finite values.
Results may differ from a plain program's by a relative error of at most 0.0023.
Values sent between devices are 32-bit elements; how exact they have to be, the bound alone decides.
A program may use at most 192 MiB of HBM per device.

v0:
```python
import jax
import jax.numpy as jnp
from jax import lax
from jax.sharding import PartitionSpec as P

ELEM = 8
ITERS = 6


reg_weight = 4.0


def shifted(value, axis, steps):
    count = lax.axis_size(axis)
    initial, last = (max(0, -steps), min(count, count - steps))
    return lax.ppermute(value, axis, [(source, source + steps) for source in range(initial, last)])


def extended(block, sides, width):
    for axis, dim in sides:
        count = lax.axis_size(axis)
        forward = [(i, i + 1) for i in range(count - 1)]
        backward = [(target, source) for source, target in forward]
        low = lax.ppermute(
            lax.slice_in_dim(block, block.shape[dim] - width, None, axis=dim), axis, forward
        )
        high = lax.ppermute(lax.slice_in_dim(block, 0, width, axis=dim), axis, backward)
        block = jnp.concatenate([low, block, high], axis=dim)
    return block


def edge_weights():
    return jnp.arange(ELEM, dtype=jnp.float32) / ELEM


def interpolate(padded):
    weights = edge_weights()
    lower_w = 1.0 - weights
    comps, nodes_z, nodes_y, nodes_x = padded.shape
    depth_direction = (
        padded[:, :-1, None] * lower_w[:, None, None] + padded[:, 1:, None] * weights[:, None, None]
    )
    depth_direction = depth_direction.reshape(comps, (nodes_z - 1) * ELEM, nodes_y, nodes_x)
    along_y = (
        depth_direction[:, :, :-1, None] * lower_w[:, None]
        + depth_direction[:, :, 1:, None] * weights[:, None]
    )
    along_y = along_y.reshape(comps, (nodes_z - 1) * ELEM, (nodes_y - 1) * ELEM, nodes_x)
    along_x = along_y[..., :-1, None] * lower_w + along_y[..., 1:, None] * weights
    return along_x.reshape(comps, (nodes_z - 1) * ELEM, (nodes_y - 1) * ELEM, (nodes_x - 1) * ELEM)


def laplacian(padded):
    centre = padded[:, 1:-1, 1:-1, 1:-1]
    beside = padded[:, :-2, 1:-1, 1:-1] + padded[:, 2:, 1:-1, 1:-1]
    beside = beside + padded[:, 1:-1, :-2, 1:-1] + padded[:, 1:-1, 2:, 1:-1]
    beside = beside + padded[:, 1:-1, 1:-1, :-2] + padded[:, 1:-1, 1:-1, 2:]
    return 6.0 * centre - beside


def collapse_width(field):
    weights = edge_weights()
    comps, zcount, ycount, xcount = field.shape
    blocks = field.reshape(comps, zcount, ycount, xcount // ELEM, ELEM)
    lower = jnp.sum(blocks * (1.0 - weights), -1)
    upper = jnp.sum(blocks * weights, -1)
    return lower + jnp.concatenate([jnp.zeros_like(upper[..., :1]), upper[..., :-1]], -1)


def reduce_y(field):
    weights = edge_weights()
    comps, zcount, ycount, xcount = field.shape
    blocks = field.reshape(comps, zcount, ycount // ELEM, ELEM, xcount)
    lower = jnp.sum(blocks * (1.0 - weights)[:, None], 3)
    upper = jnp.sum(blocks * weights[:, None], 3)
    return (lower, upper)


def reduce_z(field):
    weights = edge_weights()
    comps, zcount, ycount, xcount = field.shape
    blocks = field.reshape(comps, zcount // ELEM, ELEM, ycount, xcount)
    lower = jnp.sum(blocks * (1.0 - weights)[:, None, None], 2)
    upper = jnp.sum(blocks * weights[:, None, None], 2)
    return (lower, upper)


def assemble(field):
    nodes_x = collapse_width(field)
    lower, upper = reduce_y(nodes_x)
    carried = shifted(upper[:, :, -1:], "plane", 1)
    nodes_y = lower + jnp.concatenate([carried, upper[:, :, :-1]], 2)
    lower, upper = reduce_z(nodes_y)
    carried = shifted(upper, "slab", 1)
    return lower + jnp.concatenate([carried, upper[:, :-1]], 1)


def gradient(padded, margin, zcount, ycount, xcount):

    def piece(off_z, off_y, off_x):
        return padded[
            margin + off_z : margin + off_z + zcount,
            margin + off_y : margin + off_y + ycount,
            margin + off_x : margin + off_x + xcount,
        ]

    grad_z = (
        piece(-2, 0, 0) - 8.0 * piece(-1, 0, 0) + 8.0 * piece(1, 0, 0) - piece(2, 0, 0)
    ) / 12.0
    gradient_height = (
        piece(0, -2, 0) - 8.0 * piece(0, -1, 0) + 8.0 * piece(0, 1, 0) - piece(0, 2, 0)
    ) / 12.0
    grad_x = (
        piece(0, 0, -2) - 8.0 * piece(0, 0, -1) + 8.0 * piece(0, 0, 1) - piece(0, 0, 2)
    ) / 12.0
    return jnp.stack([grad_z, gradient_height, grad_x])


def voxel_codes(shifts):
    codes = (shifts[0] + 1) * 9 + (shifts[1] + 1) * 3 + (shifts[2] + 1)
    elem_z, elem_y, elem_x = codes.shape
    spread = jnp.broadcast_to(
        codes[:, None, :, None, :, None], (elem_z, ELEM, elem_y, ELEM, elem_x, ELEM)
    )
    return spread.reshape(elem_z * ELEM, elem_y * ELEM, elem_x * ELEM)


def warp_image(padded, margin, codes):
    zcount, ycount, xcount = codes.shape
    result = jnp.zeros(codes.shape, padded.dtype)
    for candidate in range(27):
        off_z = candidate // 9 - 1
        off_y = candidate // 3 % 3 - 1
        off_x = candidate % 3 - 1
        piece = padded[
            margin + off_z : margin + off_z + zcount,
            margin + off_y : margin + off_y + ycount,
            margin + off_x : margin + off_x + xcount,
        ]
        result = jnp.where(codes == candidate, piece, result)
    return result


def rim_nodes(vector):
    return extended(vector, (("slab", 1), ("plane", 2)), 1)


def node_parts(vector):
    rimmed = rim_nodes(vector)
    upper_side = jnp.pad(rimmed[:, 1:, 1:, :], ((0, 0), (0, 0), (0, 0), (0, 1)))
    both_sides = jnp.pad(rimmed, ((0, 0), (0, 0), (0, 0), (1, 1)))
    return (interpolate(upper_side), laplacian(both_sides))


def residual_norm(residual, counted):
    return lax.psum(jnp.sum(residual * residual * counted), ("slab", "plane"))


def body(images, shifts, initial_displacement):
    plane_count = images.shape[1]
    row_count = images.shape[2]
    column_count = images.shape[3]
    codes = voxel_codes(shifts)
    rimmed = extended(images, (("slab", 1), ("plane", 2)), 2)
    rimmed = jnp.pad(rimmed, ((0, 0), (0, 0), (0, 0), (2, 2)))
    grads = gradient(rimmed[0], 2, plane_count, row_count, column_count)
    warped = warp_image(rimmed[1], 2, codes)
    energy = lax.psum(jnp.sum(grads * grads), ("slab", "plane"))
    voxel_total = (
        plane_count * row_count * column_count * lax.axis_size("slab") * lax.axis_size("plane")
    )
    smoothing_penalty = reg_weight * energy / voxel_total
    counted = 1.0
    moved, lap_start = node_parts(initial_displacement)
    mismatch = images[0] - warped - jnp.sum(grads * moved, 0)
    rhs = assemble(grads * mismatch[None]) - smoothing_penalty * lap_start
    step = jnp.zeros_like(rhs)
    residual = rhs
    direction = rhs
    norm_now = residual_norm(residual, counted)
    for sweep in range(ITERS):
        flow, lap_part = node_parts(direction)
        scalar = jnp.sum(grads * flow, 0)
        applied = assemble(grads * scalar[None]) + smoothing_penalty * lap_part
        step_size = norm_now / lax.psum(jnp.sum(direction * applied * counted), ("slab", "plane"))
        step = step + step_size * direction
        residual = residual - step_size * applied
        norm_next = residual_norm(residual, counted)
        direction = residual + norm_next / norm_now * direction
        norm_now = norm_next
    return (initial_displacement + step, mismatch)


def solution(mesh):
    in_specs = (
        P(None, "slab", "plane", None),
        P(None, "slab", "plane", None),
        P(None, "slab", "plane", None),
    )
    out_specs = (P(None, "slab", "plane", None), P("slab", "plane", None))
    return jax.shard_map(body, mesh=mesh, in_specs=in_specs, out_specs=out_specs, check_vma=False)
```

profile of v0, /device:TPU:0, one launch (start us, length us, event | category | flops | bytes accessed | tf_op | source)
XLA Modules:
  0.0 956.9 jit_solution(6989842784682503352)
XLA Ops:
  2.1 5.5 collective-permute-start.4
  9.3 4.8 collective-permute-start
  16.4 2.7 copy.524
  66.6 3.6 collective-permute-start.9
  72.8 3.6 collective-permute-start.2
  77.1 6.7 copy.423
  83.8 6.6 copy.424
  90.4 6.5 copy.422
  97.0 19.2 %select_maximum_fusion = f32[2,12,20,1028]{2,3,1,0:T(8,128)} fusion(f32[2,12,2,1024]{2,3,1,0:T(8,128)} %copy.424, f32[2,12,16,1024]{2,3,1,0:T(8,128)} %copy.423, f32[2,12,2,1024]{2,3,1,0:T(8,128)} %copy.422), kind=kLoop, calls=%fused_computation.2 | loop fusion | flops 3947520 | bytes 3939840 | tf_op jit(solution)/shard_map/concatenate | solution.py:28
  116.1 8.1 slice_bitcast_fusion.1
  124.2 14.7 %fusion.34 = (f32[8,16,1024]{1,2,0:T(8,128)}, f32[8,16,1024]{1,2,0:T(8,128)}, f32[8,16,1024]{1,2,0:T(8,128)}) fusion(f32[12,20,1028]{1,2,0:T(8,128)S(1)} %get-tuple-element.81), kind=kLoop, calls=%fused_computation.49 | loop fusion | flops 2359296 | bytes 7864320 | tf_op jit(solution)/shard_map/div | solution.py:107
  138.9 2.8 copy.427
  141.7 2.8 copy.426
  144.5 2.8 copy.425
  147.9 2.7 copy.459
  150.7 58.9 %fusion.27 = f32[8,16,1024]{1,2,0:T(8,128)} fusion(f32[12,20,1028]{1,2,0:T(8,128)} %get-tuple-element.82, f32[8,16,128,8]{1,3,2,0:T(8,128)} %copy.459, f32[1,8,16,1024]{2,3,1,0:T(8,128)} %copy.524, pred[16,1024]{0,1:T(8,128)(4,1)S(1)} %copy.455, pred[16,1024]{0,1:T(8,128)(4,1)S(1)} %copy-done.2, pred[16,1024]{0,1:T(8,128)(4,1)S(1)} %copy-done.3, ...), kind=kLoop, calls=%fused_computation.35 | loop fusion | flops 3801088 | bytes 16171008 | tf_op jit(solution)/shard_map/sub | solution.py:175
  209.6 2.8 copy.460
  216.0 2.8 pad_add_fusion.6
  220.9 3.6 collective-permute-start.7
  224.5 2.8 copy.469
  227.3 2.8 copy.468
  230.1 2.8 copy.467
  234.1 4.8 collective-permute-start.8
  239.7 39.8 %psum.91 = f32[]{:T(128)} all-reduce(f32[]{:T(128)} %fusion.37), channel_id=1, replica_groups=mesh['slab'=4,'plane'=8] {'slab','plane'}, use_global_device_ids=true, to_apply=%region_8.9 | all-reduce | flops 1 | bytes 8 | tf_op jit(solution)/shard_map/psum | solution.py:168
  282.2 4.8 collective-permute-start.10
  297.0 2.8 pad_add_fusion.5
  301.9 2.4 collective-permute-start.13
  304.3 1.9 collective-permute-start.15
  306.3 4.8 collective-permute-start.14
  313.2 43.0 %all-reduce.22 = (f32[]{:T(128)}, f32[]{:T(128)}) all-reduce(f32[]{:T(128)} %get-tuple-element.61, f32[]{:T(128)} %get-tuple-element.60), channel_id=1, replica_groups=mesh['slab'=4,'plane'=8] {'slab','plane'}, use_global_device_ids=true, to_apply=%region_10.11 | all-reduce | flops 2 | bytes 16 | tf_op jit(solution)/shard_map/psum | solution.py:156
  358.1 41.0 %psum.94 = f32[]{:T(128)} all-reduce(f32[]{:T(128)} %multiply_reduce_fusion.43), channel_id=1, replica_groups=mesh['slab'=4,'plane'=8] {'slab','plane'}, use_global_device_ids=true, to_apply=%region_21.22 | all-reduce | flops 1 | bytes 8 | tf_op jit(solution)/shard_map/psum | solution.py:156
  401.8 4.8 collective-permute-start.16
  416.7 2.8 pad_add_fusion.4
  421.6 3.1 collective-permute-start.19
  424.7 1.9 collective-permute-start.21
  426.8 4.8 collective-permute-start.20
  433.6 42.4 %psum.95 = f32[]{:T(128)} all-reduce(f32[]{:T(128)} %get-tuple-element.76), channel_id=1, replica_groups=mesh['slab'=4,'plane'=8] {'slab','plane'}, use_global_device_ids=true, to_apply=%region_30.31 | all-reduce | flops 1 | bytes 8 | tf_op jit(solution)/shard_map/psum | solution.py:185
  478.0 40.9 %psum.96 = f32[]{:T(128)} all-reduce(f32[]{:T(128)} %get-tuple-element.74), channel_id=1, replica_groups=mesh['slab'=4,'plane'=8] {'slab','plane'}, use_global_device_ids=true, to_apply=%region_32.33 | all-reduce | flops 1 | bytes 8 | tf_op jit(solution)/shard_map/psum | solution.py:156
  521.5 4.8 collective-permute-start.22
  536.4 2.8 pad_add_fusion.3
  541.3 3.4 collective-permute-start.25
  544.7 1.9 collective-permute-start.27
  546.8 4.8 collective-permute-start.26
  553.6 42.1 %psum.97 = f32[]{:T(128)} all-reduce(f32[]{:T(128)} %get-tuple-element.72), channel_id=1, replica_groups=mesh['slab'=4,'plane'=8] {'slab','plane'}, use_global_device_ids=true, to_apply=%region_41.42 | all-reduce | flops 1 | bytes 8 | tf_op jit(solution)/shard_map/psum | solution.py:185
  597.6 41.1 %psum.98 = f32[]{:T(128)} all-reduce(f32[]{:T(128)} %get-tuple-element.70), channel_id=1, replica_groups=mesh['slab'=4,'plane'=8] {'slab','plane'}, use_global_device_ids=true, to_apply=%region_43.44 | all-reduce | flops 1 | bytes 8 | tf_op jit(solution)/shard_map/psum | solution.py:156
  641.4 4.8 collective-permute-start.28
  656.2 2.8 pad_add_fusion.2
  661.2 3.3 collective-permute-start.31
  664.5 1.9 collective-permute-start.33
  666.5 4.8 collective-permute-start.32
  673.4 42.0 %psum.99 = f32[]{:T(128)} all-reduce(f32[]{:T(128)} %get-tuple-element.68), channel_id=1, replica_groups=mesh['slab'=4,'plane'=8] {'slab','plane'}, use_global_device_ids=true, to_apply=%region_52.53 | all-reduce | flops 1 | bytes 8 | tf_op jit(solution)/shard_map/psum | solution.py:185
  717.4 41.1 %psum.100 = f32[]{:T(128)} all-reduce(f32[]{:T(128)} %get-tuple-element.66), channel_id=1, replica_groups=mesh['slab'=4,'plane'=8] {'slab','plane'}, use_global_device_ids=true, to_apply=%region_54.55 | all-reduce | flops 1 | bytes 8 | tf_op jit(solution)/shard_map/psum | solution.py:156
  761.2 4.8 collective-permute-start.34
  776.0 2.8 pad_add_fusion.1
  780.9 3.3 collective-permute-start.37
  784.2 1.9 collective-permute-start.39
  786.3 4.8 collective-permute-start.38
  793.1 42.1 %psum.101 = f32[]{:T(128)} all-reduce(f32[]{:T(128)} %get-tuple-element.64), channel_id=1, replica_groups=mesh['slab'=4,'plane'=8] {'slab','plane'}, use_global_device_ids=true, to_apply=%region_63.64 | all-reduce | flops 1 | bytes 8 | tf_op jit(solution)/shard_map/psum | solution.py:185
  837.1 41.1 %psum.102 = f32[]{:T(128)} all-reduce(f32[]{:T(128)} %multiply_reduce_fusion.35), channel_id=1, replica_groups=mesh['slab'=4,'plane'=8] {'slab','plane'}, use_global_device_ids=true, to_apply=%region_65.66 | all-reduce | flops 1 | bytes 8 | tf_op jit(solution)/shard_map/psum | solution.py:156
  880.9 4.8 collective-permute-start.40
  896.8 3.3 collective-permute-start.43
  902.2 4.8 collective-permute-start.44
  909.1 3.5 copy.509
  912.6 42.1 %psum.103 = f32[]{:T(128)} all-reduce(f32[]{:T(128)} %fusion.103), channel_id=1, replica_groups=mesh['slab'=4,'plane'=8] {'slab','plane'}, use_global_device_ids=true, to_apply=%region_74.75 | all-reduce | flops 1 | bytes 8 | tf_op jit(solution)/shard_map/psum | solution.py:185
  (466 shorter events, 161.3 us)
Async XLA Ops:
  0.6 24.7 %collective-permute-start.5 = (f32[3,1,2,128]{3,2,0,1:T(2,128)}, f32[3,1,2,128]{3,2,0,1:T(2,128)S(1)}, u32[]{:S(2)}, u32[]{:S(2)}) collective-permute-start(f32[3,1,2,128]{3,2,0,1:T(2,128)} %bitcast.337), channel_id=1, source_target_pairs={{8,0},{16,8},{24,16},{9,1},{17,9},{25,17},{10,2},{18,10},{26,18},{... | collective-permute-start | bytes 9224 | tf_op jit(solution)/shard_map/ppermute | solution.py:27
  2.1 23.2 %collective-permute-start.4 = (f32[3,1,2,128]{3,2,0,1:T(2,128)}, f32[3,1,2,128]{3,2,0,1:T(2,128)S(1)}, u32[]{:S(2)}, u32[]{:S(2)}) collective-permute-start(f32[3,1,2,128]{3,2,0,1:T(2,128)} %bitcast.338), channel_id=1, source_target_pairs={{0,8},{8,16},{16,24},{1,9},{9,17},{17,25},{2,10},{10,18},{18,26},{... | collective-permute-start | bytes 9224 | tf_op jit(solution)/shard_map/ppermute | solution.py:24
  9.3 61.8 %collective-permute-start = (f32[2,2,16,1024]{3,2,1,0:T(8,128)S(1)}, f32[2,2,16,1024]{3,2,1,0:T(8,128)S(1)}, u32[]{:S(2)}, u32[]{:S(2)}) collective-permute-start(f32[2,2,16,1024]{3,2,1,0:T(8,128)S(1)} %get-tuple-element.89), channel_id=1, source_target_pairs={{0,8},{8,16},{16,24},{1,9},{9,17},{17,25},{2,10},{10,18},{18,26},{... | collective-permute-start | bytes 786440 | tf_op jit(solution)/shard_map/ppermute | solution.py:24
  14.2 57.1 %collective-permute-start.1 = (f32[2,2,16,1024]{3,2,1,0:T(8,128)}, f32[2,2,16,1024]{3,2,1,0:T(8,128)S(1)}, u32[]{:S(2)}, u32[]{:S(2)}) collective-permute-start(f32[2,2,16,1024]{3,2,1,0:T(8,128)} %get-tuple-element.88), channel_id=1, source_target_pairs={{8,0},{16,8},{24,16},{9,1},{17,9},{25,17},{10,2},{18,10},{26,18},{... | collective-permute-start | bytes 786440 | tf_op jit(solution)/shard_map/ppermute | solution.py:27
  25.3 213.5 %copy-start.25 = (f32[3,1,2,128]{3,2,0,1:T(2,128)}, f32[3,1,2,128]{3,2,0,1:T(2,128)S(1)}, u32[]{:S(2)}) copy-start(f32[3,1,2,128]{3,2,0,1:T(2,128)S(1)} %collective-permute-done.5) | copy-start | bytes 9220
  26.0 44.2 %collective-permute-start.6 = (f32[3,3,1,128]{3,2,0,1:T(1,128)S(1)}, f32[3,3,1,128]{3,2,0,1:T(1,128)S(1)}, u32[]{:S(2)}, u32[]{:S(2)}) collective-permute-start(f32[3,3,1,128]{3,2,0,1:T(1,128)S(1)} %get-tuple-element.159), channel_id=1, source_target_pairs={{1,0},{2,1},{3,2},{4,3},{5,4},{6,5},{7,6},{9,8},{10,9},{11,10},{12... | collective-permute-start | bytes 13832 | tf_op jit(solution)/shard_map/ppermute | solution.py:27
  66.6 172.3 %collective-permute-start.9 = (f32[3,3,1,128]{3,2,0,1:T(1,128)}, f32[3,3,1,128]{3,2,0,1:T(1,128)}, u32[]{:S(2)}, u32[]{:S(2)}) collective-permute-start(f32[3,3,1,128]{3,2,0,1:T(1,128)} %get-tuple-element.158), channel_id=1, source_target_pairs={{0,1},{1,2},{2,3},{3,4},{4,5},{5,6},{6,7},{8,9},{9,10},{10,11},{11... | collective-permute-start | bytes 13832 | tf_op jit(solution)/shard_map/ppermute | solution.py:24
  71.5 12.4 %collective-permute-start.3 = (f32[2,12,2,1024]{3,2,1,0:T(2,128)S(1)}, f32[2,12,2,1024]{3,2,1,0:T(2,128)S(1)}, u32[]{:S(2)}, u32[]{:S(2)}) collective-permute-start(f32[2,12,2,1024]{3,2,1,0:T(2,128)S(1)} %get-tuple-element.87), channel_id=1, source_target_pairs={{1,0},{2,1},{3,2},{4,3},{5,4},{6,5},{7,6},{9,8},{10,9},{11,10},{12... | collective-permute-start | bytes 589832 | tf_op jit(solution)/shard_map/ppermute | solution.py:27
  72.8 17.7 %collective-permute-start.2 = (f32[2,12,2,1024]{3,2,1,0:T(2,128)S(1)}, f32[2,12,2,1024]{3,2,1,0:T(2,128)S(1)}, u32[]{:S(2)}, u32[]{:S(2)}) collective-permute-start(f32[2,12,2,1024]{3,2,1,0:T(2,128)S(1)} %get-tuple-element.86), channel_id=1, source_target_pairs={{0,1},{1,2},{2,3},{3,4},{4,5},{5,6},{6,7},{8,9},{9,10},{10,11},{11... | collective-permute-start | bytes 589832 | tf_op jit(solution)/shard_map/ppermute | solution.py:24
  220.9 13.1 %collective-permute-start.7 = (f32[3,8,1,128]{3,1,2,0:T(8,128)S(1)}, f32[3,8,1,128]{3,1,2,0:T(8,128)S(1)}, u32[]{:S(2)}, u32[]{:S(2)}) collective-permute-start(f32[3,8,1,128]{3,1,2,0:T(8,128)S(1)} %bitcast.350), channel_id=1, source_target_pairs={{0,1},{1,2},{2,3},{3,4},{4,5},{5,6},{6,7},{8,9},{9,10},{10,11},{11... | collective-permute-start | bytes 36872 | tf_op jit(solution)/shard_map/ppermute | solution.py:16
  232.9 59.8 %copy-start.63 = (f32[16]{0:T(128)S(1)}, f32[16]{0:T(128)}, u32[]{:S(2)}) copy-start(f32[16]{0:T(128)} %copy-done.62) | copy-start | bytes 196
  232.9 59.8 %copy-start.70 = (f32[16]{0:T(128)S(1)}, f32[16]{0:T(128)}, u32[]{:S(2)}) copy-start(f32[16]{0:T(128)} %copy-done.69) | copy-start | bytes 196
  234.1 46.0 %collective-permute-start.8 = (f32[3,1,2,128]{3,2,0,1:T(2,128)S(1)}, f32[3,1,2,128]{3,2,0,1:T(2,128)S(1)}, u32[]{:S(2)}, u32[]{:S(2)}) collective-permute-start(f32[3,1,2,128]{3,2,0,1:T(2,128)S(1)} %bitcast.357), channel_id=1, source_target_pairs={{0,8},{8,16},{16,24},{1,9},{9,17},{17,25},{2,10},{10,18},{18,26},{... | collective-permute-start | bytes 9224 | tf_op jit(solution)/shard_map/ppermute | solution.py:16
  280.9 6.1 collective-permute-start.11
  282.2 6.1 collective-permute-start.10
  288.9 3.0 collective-permute-start.12
  299.7 112.7 %copy-start.64 = (f32[16]{0:T(128)S(1)}, f32[16]{0:T(128)}, u32[]{:S(2)}) copy-start(f32[16]{0:T(128)} %copy-done.62) | copy-start | bytes 196
  299.7 112.7 %copy-start.71 = (f32[16]{0:T(128)S(1)}, f32[16]{0:T(128)}, u32[]{:S(2)}) copy-start(f32[16]{0:T(128)} %copy-done.69) | copy-start | bytes 196
  301.9 4.4 collective-permute-start.13
  304.3 6.9 collective-permute-start.15
  306.3 6.1 collective-permute-start.14
  313.2 99.1 %copy-start.21 = (f32[3,1,2,128]{3,2,0,1:T(2,128)}, f32[3,1,2,128]{3,2,0,1:T(2,128)S(1)}, u32[]{:S(2)}) copy-start(f32[3,1,2,128]{3,2,0,1:T(2,128)S(1)} %get-tuple-element.78) | copy-start | bytes 9220
  400.5 6.1 collective-permute-start.17
  401.8 6.1 collective-permute-start.16
  408.6 3.0 collective-permute-start.18
  419.4 57.9 %copy-start.22 = (f32[3,1,2,128]{3,2,0,1:T(2,128)S(1)}, f32[3,1,2,128]{3,2,0,1:T(2,128)}, u32[]{:S(2)}) copy-start(f32[3,1,2,128]{3,2,0,1:T(2,128)} %copy-done.21) | copy-start | bytes 9220
  419.4 112.7 %copy-start.65 = (f32[16]{0:T(128)S(1)}, f32[16]{0:T(128)}, u32[]{:S(2)}) copy-start(f32[16]{0:T(128)} %copy-done.62) | copy-start | bytes 196
  419.5 112.7 %copy-start.72 = (f32[16]{0:T(128)S(1)}, f32[16]{0:T(128)}, u32[]{:S(2)}) copy-start(f32[16]{0:T(128)} %copy-done.69) | copy-start | bytes 196
  421.6 5.1 collective-permute-start.19
  424.7 6.9 collective-permute-start.21
  426.8 6.1 collective-permute-start.20
  520.2 6.1 collective-permute-start.23
  521.5 6.1 collective-permute-start.22
  528.3 3.0 collective-permute-start.24
  539.2 57.9 %copy-start.59 = (f32[3,1,2,128]{3,2,0,1:T(2,128)S(1)}, f32[3,1,2,128]{3,2,0,1:T(2,128)}, u32[]{:S(2)}) copy-start(f32[3,1,2,128]{3,2,0,1:T(2,128)} %copy-done.58) | copy-start | bytes 9220
  539.2 112.8 %copy-start.66 = (f32[16]{0:T(128)S(1)}, f32[16]{0:T(128)}, u32[]{:S(2)}) copy-start(f32[16]{0:T(128)} %copy-done.62) | copy-start | bytes 196
  539.2 112.8 %copy-start.73 = (f32[16]{0:T(128)S(1)}, f32[16]{0:T(128)}, u32[]{:S(2)}) copy-start(f32[16]{0:T(128)} %copy-done.69) | copy-start | bytes 196
  541.3 5.4 collective-permute-start.25
  544.7 6.9 collective-permute-start.27
  546.8 6.1 collective-permute-start.26
  640.1 6.1 collective-permute-start.29
  641.4 6.1 collective-permute-start.28
  648.1 3.0 collective-permute-start.30
  659.0 57.7 %copy-start.61 = (f32[3,1,2,128]{3,2,0,1:T(2,128)S(1)}, f32[3,1,2,128]{3,2,0,1:T(2,128)}, u32[]{:S(2)}) copy-start(f32[3,1,2,128]{3,2,0,1:T(2,128)} %copy-done.60) | copy-start | bytes 9220
  659.0 112.7 %copy-start.67 = (f32[16]{0:T(128)S(1)}, f32[16]{0:T(128)}, u32[]{:S(2)}) copy-start(f32[16]{0:T(128)} %copy-done.62) | copy-start | bytes 196
  659.1 112.7 %copy-start.74 = (f32[16]{0:T(128)S(1)}, f32[16]{0:T(128)}, u32[]{:S(2)}) copy-start(f32[16]{0:T(128)} %copy-done.69) | copy-start | bytes 196
  661.2 5.3 collective-permute-start.31
  664.5 6.9 collective-permute-start.33
  666.5 6.1 collective-permute-start.32
  759.9 6.1 collective-permute-start.35
  761.2 6.1 collective-permute-start.34
  767.9 3.0 collective-permute-start.36
  778.8 57.6 %copy-start.24 = (f32[3,1,2,128]{3,2,0,1:T(2,128)S(1)}, f32[3,1,2,128]{3,2,0,1:T(2,128)}, u32[]{:S(2)}) copy-start(f32[3,1,2,128]{3,2,0,1:T(2,128)} %copy-done.23) | copy-start | bytes 9220
  778.8 111.4 %copy-start.68 = (f32[16]{0:T(128)S(1)}, f32[16]{0:T(128)}, u32[]{:S(2)}) copy-start(f32[16]{0:T(128)} %copy-done.62) | copy-start | bytes 196
  778.8 111.4 %copy-start.75 = (f32[16]{0:T(128)S(1)}, f32[16]{0:T(128)}, u32[]{:S(2)}) copy-start(f32[16]{0:T(128)} %copy-done.69) | copy-start | bytes 196
  780.9 5.2 collective-permute-start.37
  784.2 6.9 collective-permute-start.39
  786.3 6.1 collective-permute-start.38
  879.6 6.1 collective-permute-start.41
  880.9 6.1 collective-permute-start.40
  887.0 3.1 collective-permute-start.42
  896.8 5.2 collective-permute-start.43
  900.1 6.9 collective-permute-start.45
  902.2 6.1 collective-permute-start.44
  (64 other events, 833.3 us)
where the time goes:
time: 964 us; the launch traced here: 957 us
  blocking collectives  499 us (52%)
  local copies, waits for them, and re-layouts  140 us (15%)
  other arithmetic  139 us (14%)
  starting transfers between devices  136 us (14%)
  waiting for transfers between devices  24.5 us (3%)
  between operations  18.8 us (2%)
    psum x6, blocking collectives, residual_norm(): return lax.psum(jnp.sum(residual * residual * counted), ('slab', 'plane'))  248 us
    psum x5, blocking collectives, body(): lax.psum(jnp.sum(direction * applied * counted), ('slab', 'plane'))  211 us
    sub x1, other arithmetic, body(): mismatch = images[0] - warped - jnp.sum(grads * moved, 0)  58.9 us
    ppermute x16, starting transfers between devices, extended(): lax.ppermute(lax.slice_in_dim(block, block.shape[dim] - width, None, axis...  58 us
    ppermute x14, starting transfers between devices, shifted(): lax.ppermute(value, axis, [(source, source + steps) for source in range(i...  56.1 us
    eq x54, local copies, waits for them, and re-layouts, warp_image(): result = jnp.where(codes == candidate, piece, result)  40.7 us
    psum x1, blocking collectives, body(): energy = lax.psum(jnp.sum(grads * grads), ('slab', 'plane'))  39.8 us
    unnamed x180, local copies, waits for them, and re-layouts  24.2 us
  transfers between devices with their start and end apart: 46, of which 18 were waited for; matrix products, arithmetic and copies ran while one was open for 22% of the time, Pallas kernels for 0%

commit v1 on v0

v1 whole, which is shorter than its diff:
```python
import functools

import jax
import jax.numpy as jnp
import ml_dtypes
import numpy as np
from jax import lax
from jax.experimental import pallas as pl
from jax.experimental.pallas import tpu as pltpu
from jax.sharding import PartitionSpec as P

ITERS = 6
reg_weight = 4.0

MESH = pl.DeviceIdType.MESH
F32 = jnp.float32
BF16 = jnp.bfloat16
TILE = 8
COMPS = 3
PAIRS = ((0, 0), (0, 1), (0, 2), (1, 1), (1, 2), (2, 2))
AROUND = tuple((dz, dy) for dz in (-1, 0, 1) for dy in (-1, 0, 1) if (dz, dy) != (0, 0))


def place_of(dz, dy):
    return (dz + 1) * 3 + dy + 1


def pair_of(i, j):
    return PAIRS.index((min(i, j), max(i, j)))


def matrices(elem, rows, across):
    w = np.arange(elem) / elem
    squares = ((1 - w) ** 2, w * (1 - w), w**2)
    count = elem * across
    hats = np.zeros((count, across))
    stencil = np.zeros((count, 2 * across))
    spread = np.zeros((across, count))
    for e in range(across):
        at = slice(e * elem, (e + 1) * elem)
        spread[e, at] = 1
        hats[at, e] = 1 - w
        stencil[at, e] += squares[0]
        if e + 1 < across:
            hats[at, e + 1] = w
            stencil[at, e + 1] += squares[2]
            stencil[at, across + e] = squares[1]

    height = rows * elem
    depth = len(PAIRS) * 3 * height

    def column(ij, cz, row):
        start = (ij * 3 + cz) * height + row * elem
        return slice(start, start + elem)

    last = rows - 1
    slab_rows = [(ij, cz, cy, r) for ij in range(6) for cz in (1, 2) for cy in range(3) for r in range(rows)]
    plane_rows = [(ij, cz, cy, last) for ij in range(6) for cz in (0, 1) for cy in (1, 2)]
    diag_rows = [(ij, cz, cy, last) for ij in range(6) for cz in (1, 2) for cy in (1, 2)]
    parts = []
    start = 0
    for listed in (slab_rows, plane_rows, diag_rows):
        used = -(-len(listed) // TILE) * TILE
        parts.append((start, used))
        start += used + TILE
    total = start
    send = np.zeros((total, depth))
    index = [{}, {}, {}]
    for part, listed in enumerate((slab_rows, plane_rows, diag_rows)):
        for n, key in enumerate(listed):
            ij, cz, cy, r = key
            send[parts[part][0] + n, column(ij, cz, r)] = squares[cy]
            index[part][key] = parts[part][0] + n

    own = np.zeros((COMPS * 9 * TILE, depth))
    came = np.zeros((COMPS * 9 * TILE, total))
    for i in range(COMPS):
        for dz in (-1, 0, 1):
            for dy in (-1, 0, 1):
                for j in range(COMPS):
                    for r in range(rows):
                        out = (i * 9 + place_of(dz, dy)) * TILE + j * rows + r
                        ij = pair_of(i, j)
                        layers = {0: ((0, 0), (-1, 2)), 1: ((0, 1),), -1: ((-1, 1),)}[dz]
                        lines = {0: ((r, 0), (r - 1, 2)), 1: ((r, 1),), -1: ((r - 1, 1),)}[dy]
                        for layer, cz in layers:
                            for line, cy in lines:
                                if layer == 0 and line >= 0:
                                    own[out, column(ij, cz, line)] = squares[cy]
                                elif layer < 0 and line >= 0:
                                    came[out, index[0][(ij, cz, cy, line)]] = 1
                                elif layer == 0:
                                    came[out, index[1][(ij, cz, cy, last)]] = 1
                                else:
                                    came[out, index[2][(ij, cz, cy, last)]] = 1

    loads = np.zeros((4 * TILE, COMPS * 2 * height))

    def line_of(i, cz, row):
        start = (i * 2 + cz) * height + row * elem
        return slice(start, start + elem)

    for i in range(COMPS):
        for r in range(rows):
            out = i * rows + r
            for cz in (0, 1):
                loads[cz * TILE + out, line_of(i, cz, r)] = 1 - w
                if r > 0:
                    loads[cz * TILE + out, line_of(i, cz, r - 1)] = w
        for cz in (0, 1):
            loads[(2 + cz) * TILE + i * rows, line_of(i, cz, last)] = w
    arrays = (stencil, hats, hats.T, spread, send, own, came, loads)
    return parts, [np.asarray(a, dtype=ml_dtypes.bfloat16) for a in arrays]


def split(x):
    high = x.astype(BF16)
    return high, (x - high.astype(F32)).astype(BF16)


def dot(a, b):
    return jnp.dot(a, b, preferred_element_type=F32)


def dot_left(x, exact):
    high, low = split(x)
    return dot(high, exact) + dot(low, exact)


def dot_right(exact, x):
    high, low = split(x)
    return dot(exact, high) + dot(exact, low)


def kernel(
    slabs,
    planes,
    parts,
    images,
    shifts,
    start_field,
    w_stencil,
    w_hats,
    w_nodes,
    w_spread,
    w_send,
    w_own,
    w_came,
    w_loads,
    out_field,
    out_mismatch,
    ref_ext,
    def_ext,
    pack,
    got_rows,
    got_diag,
    tiles,
    halo,
    dots,
    grads,
    mis,
    nodes_x,
    moves,
    moments,
    loads,
    send_buf,
    got_buf,
    coefs,
    res,
    img,
    load_sem,
    out_sem,
    face_send,
    face_recv,
    row_send,
    row_recv,
    diag_send,
    diag_recv,
    tile_send,
    tile_recv,
    dot_send,
    dot_recv,
    part_send,
    part_recv,
):
    _, zs, ys, xs = images.shape
    rows, across = shifts.shape[2], shifts.shape[3]
    elem = xs // across
    devices = slabs * planes
    slab, plane = lax.axis_index("slab"), lax.axis_index("plane")
    me = slab * planes + plane

    def present(dz, dy):
        ok = None
        for d, at, count in ((dz, slab, slabs), (dy, plane, planes)):
            if d:
                here = at < count - 1 if d > 0 else at > 0
                ok = here if ok is None else jnp.logical_and(ok, here)
        return ok

    def beside(dz, dy):
        return (slab + dz, plane + dy)

    def other(k):
        to = lax.rem(me + k, devices)
        return (lax.div(to, planes), lax.rem(to, planes))

    mine = [
        pltpu.make_async_copy(images.at[0], ref_ext.at[pl.ds(2, zs), pl.ds(TILE, ys)], load_sem.at[0]),
        pltpu.make_async_copy(images.at[1], def_ext.at[pl.ds(1, zs), pl.ds(TILE, ys)], load_sem.at[1]),
    ]
    for copy in mine:
        copy.start()
    halo[...] = jnp.zeros(halo.shape, F32)
    tiles[...] = jnp.zeros(tiles.shape, F32)
    got_buf[...] = jnp.zeros(got_buf.shape, F32)
    for j in range(COMPS):
        tiles[0, j * rows : (j + 1) * rows, :] = start_field[j, 0]

    barrier = pltpu.get_barrier_semaphore()

    def greet(k, carry):
        pl.semaphore_signal(barrier, inc=1, device_id=other(k), device_id_type=MESH)
        return carry

    lax.fori_loop(1, devices, greet, 0)
    for copy in mine:
        copy.wait()

    for side, (far, near) in enumerate(((1, 0), (ys - 2, ys - 1))):
        pack[side, 0:zs, :] = ref_ext[2 : 2 + zs, TILE + far, :]
        pack[side, zs : 2 * zs, :] = ref_ext[2 : 2 + zs, TILE + near, :]
        pack[side, 2 * zs :, :] = def_ext[1 : 1 + zs, TILE + near, :]
    pl.semaphore_wait(barrier, devices - 1)

    def remote(src, dst, send, recv, to):
        return pltpu.make_async_remote_copy(
            src_ref=src, dst_ref=dst, send_sem=send, recv_sem=recv, device_id=to, device_id_type=MESH
        )

    def faces():
        out = []
        for n, d in enumerate((-1, 1)):
            low = 0 if d < 0 else zs - 2
            here = ref_ext.at[pl.ds(2 + low, 2), pl.ds(TILE, ys)]
            there = ref_ext.at[pl.ds(2 + zs if d < 0 else 0, 2), pl.ds(TILE, ys)]
            out.append(((d, 0), remote(here, there, face_send.at[n, 0], face_recv.at[n, 0], beside(d, 0))))
            low = 0 if d < 0 else zs - 1
            here = def_ext.at[pl.ds(1 + low, 1), pl.ds(TILE, ys)]
            there = def_ext.at[pl.ds(1 + zs if d < 0 else 0, 1), pl.ds(TILE, ys)]
            out.append(((d, 0), remote(here, there, face_send.at[n, 1], face_recv.at[n, 1], beside(d, 0))))
        for n, d in enumerate((-1, 1)):
            out.append(
                ((0, d), remote(pack.at[n], got_rows.at[n], row_send.at[n], row_recv.at[n], beside(0, d)))
            )
        for n, (dz, dy) in enumerate(((-1, -1), (-1, 1), (1, -1), (1, 1))):
            here = pack.at[(dy + 1) // 2, pl.ds(2 * zs, zs)]
            out.append(
                ((dz, dy), remote(here, got_diag.at[n], diag_send.at[n], diag_recv.at[n], beside(dz, dy)))
            )
        return out

    def around(stage):
        out = []
        for n, (dz, dy) in enumerate(AROUND):
            copy = remote(
                tiles.at[stage],
                halo.at[stage, place_of(-dz, -dy)],
                tile_send.at[stage, n],
                tile_recv.at[stage, n],
                beside(dz, dy),
            )
            out.append(((dz, dy), copy))
        return out

    def begin(copies):
        for (dz, dy), copy in copies:
            pl.when(present(dz, dy))(copy.start)

    def arrive(copies):
        for (dz, dy), copy in copies:
            pl.when(present(-dz, -dy))(copy.wait_recv)

    def sent(copies):
        for (dz, dy), copy in copies:
            pl.when(present(dz, dy))(copy.wait_send)

    def share(stage):
        def one(k, carry):
            slot = dots.at[stage, me]
            remote(slot, slot, dot_send.at[stage], dot_recv.at[stage], other(k)).start()
            return carry

        lax.fori_loop(1, devices, one, 0)

    def shared(sem, stage):
        some = dots.at[stage, pl.ds(0, devices - 1)]
        pltpu.make_async_copy(some, some, sem.at[stage]).wait()

    def totals(stage):
        shared(dot_recv, stage)
        lanes = jnp.sum(dots[stage], axis=0)
        return jnp.sum(lanes, axis=1, keepdims=True)

    image_copies = faces()
    start_copies = around(0)
    begin(image_copies)
    begin(start_copies)

    codes = jnp.concatenate([shifts[j, 0] for j in range(COMPS)], axis=0).astype(F32).astype(BF16)
    wide = dot(codes, w_spread[...])
    for n, dx in enumerate((-1, 0, 1)):
        moves[n, 0 : COMPS * rows, :] = pltpu.roll(wide, dx % xs, 1) if dx else wide

    arrive(start_copies)
    halo[0, place_of(0, 0)] = tiles[0]
    corner = jnp.concatenate([halo[0, place_of(dz, dy)] for dz in (0, 1) for dy in (0, 1)], axis=0)
    nodes_x[...] = dot_left(corner, w_nodes[...])

    arrive(image_copies)

    def clear(dz, dy, *views):
        def run():
            for ref, index in views:
                ref[index] = jnp.zeros(ref[index].shape, F32)

        pl.when(jnp.logical_not(present(dz, dy)))(run)

    clear(-1, 0, (ref_ext, (slice(0, 2),)), (def_ext, (slice(0, 1),)))
    clear(1, 0, (ref_ext, (slice(2 + zs, 4 + zs),)), (def_ext, (slice(1 + zs, 2 + zs),)))
    for n, d in enumerate((1, -1)):
        clear(0, d, (got_rows, (n,)))
    for n, (dz, dy) in enumerate(((1, 1), (1, -1), (-1, 1), (-1, -1))):
        clear(dz, dy, (got_diag, (n,)))
    top = TILE + ys
    ref_ext[2 : 2 + zs, top, :] = got_rows[0, zs : 2 * zs, :]
    ref_ext[2 : 2 + zs, top + 1, :] = got_rows[0, 0:zs, :]
    def_ext[1 : 1 + zs, top, :] = got_rows[0, 2 * zs :, :]
    ref_ext[2 : 2 + zs, TILE - 2, :] = got_rows[1, 0:zs, :]
    ref_ext[2 : 2 + zs, TILE - 1, :] = got_rows[1, zs : 2 * zs, :]
    def_ext[1 : 1 + zs, TILE - 1, :] = got_rows[1, 2 * zs :, :]
    def_ext[1 + zs, top : top + 1, :] = got_diag[0, 0:1, :]
    def_ext[1 + zs, TILE - 1 : TILE, :] = got_diag[1, 0:1, :]
    def_ext[0, top : top + 1, :] = got_diag[2, zs - 1 : zs, :]
    def_ext[0, TILE - 1 : TILE, :] = got_diag[3, zs - 1 : zs, :]

    lane = lax.broadcasted_iota(jnp.int32, (TILE, xs), 1)
    up = lax.broadcasted_iota(jnp.int32, (TILE, xs), 0).astype(F32) / elem

    def along(value, d):
        rolled = pltpu.roll(value, (-d) % xs, 1)
        inside = lane < xs - d if d > 0 else lane >= -d
        return jnp.where(inside, rolled, 0.0)

    def voxels(z, energy):
        wz = z.astype(F32) / elem
        for r in range(rows):
            base = TILE + r * elem

            def ref(dz, dy):
                return ref_ext[z + (2 + dz), base + dy : base + dy + elem, :]

            centre = ref(0, 0)
            g = [
                (ref(-2, 0) - ref(2, 0) + 8.0 * (ref(1, 0) - ref(-1, 0))) * (1.0 / 12.0),
                (ref(0, -2) - ref(0, 2) + 8.0 * (ref(0, 1) - ref(0, -1))) * (1.0 / 12.0),
                (
                    along(centre, -2)
                    - along(centre, 2)
                    + 8.0 * (along(centre, 1) - along(centre, -1))
                )
                * (1.0 / 12.0),
            ]
            warped = None
            for n, dx in enumerate((-1, 0, 1)):
                s = [moves[n, j * rows + r : j * rows + r + 1, :] for j in range(2)]
                s = [jnp.broadcast_to(v, (elem, xs)) for v in s]
                below, above = s[0] < -0.5, s[0] > 0.5
                line = []
                for dy in (-1, 0, 1):
                    at = pl.ds(base + dy, elem)
                    value = jnp.where(below, def_ext[z, at, :], def_ext[z + 1, at, :])
                    line.append(jnp.where(above, def_ext[z + 2, at, :], value))
                value = jnp.where(s[1] < -0.5, line[0], line[1])
                value = jnp.where(s[1] > 0.5, line[2], value)
                if dx:
                    value = along(value, dx)
                sx = jnp.broadcast_to(moves[1, 2 * rows + r : 2 * rows + r + 1, :], (elem, xs))
                if warped is None:
                    warped = value
                else:
                    warped = jnp.where(sx > dx - 0.5, value, warped)
            total = centre - warped
            for j in range(COMPS):

                def node(line):
                    dy = line // rows
                    at = j * rows + line % rows
                    low = nodes_x[dy * TILE + at : dy * TILE + at + 1, :]
                    high = nodes_x[(2 + dy) * TILE + at : (2 + dy) * TILE + at + 1, :]
                    return (1.0 - wz) * low + wz * high

                moved = (1.0 - up) * node(r) + up * node(r + 1)
                total = total - g[j] * moved
                grads[j, z, r * elem : (r + 1) * elem, :] = g[j]
                energy = energy + g[j] * g[j]
            mis[z, r * elem : (r + 1) * elem, :] = total
        return energy

    energy = lax.fori_loop(0, zs, voxels, jnp.zeros((TILE, xs), F32))
    store = pltpu.make_async_copy(mis, out_mismatch, out_sem)
    store.start()
    energy = jnp.sum(energy, axis=0, keepdims=True)
    dots[0, me] = jnp.zeros(dots.shape[2:], F32)
    row = energy[:, :across]
    for c in range(1, xs // across):
        row = row + energy[:, c * across : (c + 1) * across]
    dots[0, me, 0:1, :] = row
    share(0)

    width = 128
    lines = xs // width

    def gather(n, carry):
        r, c = lax.div(n, lines), lax.rem(n, lines)
        ay = pl.ds(pl.multiple_of(r * elem, elem), elem)
        ax = pl.ds(pl.multiple_of(c * width, width), width)
        sums = [[None] * 3 for _ in PAIRS]
        forces = [[None] * 2 for _ in range(COMPS)]

        def add(total, weight, value):
            if weight == 0.0:
                return total
            term = value if weight == 1.0 else weight * value
            return term if total is None else total + term

        for z in range(zs):
            w = z / elem
            g = [grads[j, z, ay, ax] for j in range(COMPS)]
            q = mis[z, ay, ax]
            for ij, (i, j) in enumerate(PAIRS):
                product = g[i] * g[j]
                for cz, weight in enumerate(((1 - w) ** 2, w * (1 - w), w * w)):
                    sums[ij][cz] = add(sums[ij][cz], weight, product)
            for i in range(COMPS):
                product = g[i] * q
                for cz, weight in enumerate((1 - w, w)):
                    forces[i][cz] = add(forces[i][cz], weight, product)
        for ij in range(len(PAIRS)):
            for cz in range(3):
                at = pl.multiple_of((ij * 3 + cz) * ys + r * elem, elem)
                moments[pl.ds(at, elem), ax] = sums[ij][cz]
        for i in range(COMPS):
            for cz in range(2):
                at = pl.multiple_of((i * 2 + cz) * ys + r * elem, elem)
                loads[pl.ds(at, elem), ax] = forces[i][cz]
        return carry

    lax.fori_loop(0, rows * lines, gather, 0)
    summed = dot_left(moments[...], w_stencil[...])
    load_tiles = dot_right(w_loads[...], dot_left(loads[...], w_hats[...]))
    send_buf[...] = dot_right(w_send[...], summed)
    for (start, used), n in zip(parts, (1, 2, 3)):
        send_buf[start + used : start + used + TILE, :across] = load_tiles[n * TILE : (n + 1) * TILE]
    part_copies = []
    for n, ((start, used), to) in enumerate(zip(parts, ((1, 0), (0, 1), (1, 1)))):
        at = pl.ds(start, used + TILE)
        part_copies.append(
            (to, remote(send_buf.at[at], got_buf.at[at], part_send.at[n], part_recv.at[n], beside(*to)))
        )
    begin(part_copies)
    coefs[...] = dot_right(w_own[...], summed)

    node_lane = lax.broadcasted_iota(jnp.int32, (TILE, across), 1)
    sub = lax.broadcasted_iota(jnp.int32, (TILE, across), 0)
    line = lax.rem(sub, rows)
    group = lax.div(sub, rows)

    def neighbour(get, dz, dy):
        centre = get(place_of(dz, 0))
        if dy == 0:
            return centre
        edge = get(place_of(dz, dy))
        inner = pltpu.roll(centre, (-dy) % TILE, 0)
        outer = pltpu.roll(edge, (dy * (rows - 1)) % TILE, 0)
        return jnp.where(line == (rows - 1 if dy > 0 else 0), outer, inner)

    def start_at(place):
        return halo[0, place]

    centre = start_at(place_of(0, 0))
    lap = 6.0 * centre - neighbour(start_at, -1, 0) - neighbour(start_at, 1, 0)
    lap = lap - neighbour(start_at, 0, -1) - neighbour(start_at, 0, 1)
    lap = lap - jnp.where(node_lane > 0, pltpu.roll(centre, 1, 1), 0.0)
    lap = lap - jnp.where(node_lane < across - 1, pltpu.roll(centre, across - 1, 1), 0.0)
    lap = jnp.where(group < COMPS, lap, 0.0)

    penalty = totals(0)[0:1, :] * (reg_weight / (devices * zs * ys * xs))
    arrive(part_copies)
    rhs = load_tiles[0:TILE] - penalty * lap
    for start, used in parts:
        rhs = rhs + got_buf[start + used : start + used + TILE, :across]
    tiles[1] = rhs
    rhs_copies = around(1)
    begin(rhs_copies)

    coefs[...] = coefs[...] + dot_right(w_came[...], got_buf[...])
    for i in range(COMPS):
        same = jnp.where(group == i, 1.0, 0.0) * penalty

        def raise_by(dz, dy, part, value):
            at = pl.ds((i * 9 + place_of(dz, dy)) * TILE, TILE)
            to = pl.ds(part * across, across)
            coefs[at, to] = coefs[at, to] + value

        raise_by(0, 0, 0, 6.0 * same)
        raise_by(0, 0, 1, jnp.where(node_lane < across - 1, -same, 0.0))
        for dz, dy in ((-1, 0), (1, 0), (0, -1), (0, 1)):
            raise_by(dz, dy, 0, -same)

    arrive(rhs_copies)
    halo[1, place_of(0, 0)] = rhs
    res[...] = halo[1]
    img[...] = jnp.zeros(img.shape, F32)

    def operate():
        out = [None] * COMPS
        back = [None] * COMPS
        for dz in (-1, 0, 1):
            for dy in (-1, 0, 1):
                v = neighbour(lambda place: res[place], dz, dy)
                ahead = pltpu.roll(v, across - 1, 1)
                for i in range(COMPS):
                    at = pl.ds((i * 9 + place_of(dz, dy)) * TILE, TILE)
                    here, link = coefs[at, 0:across], coefs[at, across : 2 * across]
                    term = here * v + link * ahead
                    out[i] = term if out[i] is None else out[i] + term
                    term = link * v
                    back[i] = term if back[i] is None else back[i] + term
        image = jnp.zeros((TILE, across), F32)
        for i in range(COMPS):
            value = out[i] + pltpu.roll(back[i], 1, 1)
            value = value + pltpu.roll(value, TILE // 2, 0)
            value = value + pltpu.roll(value, rows, 0)
            image = jnp.where(group == i, value, image)
        return image

    direction = jnp.zeros((TILE, across), F32)
    step = jnp.zeros((TILE, across), F32)
    norm_before = size_before = None
    copies = [image_copies, start_copies, part_copies, rhs_copies]
    for k in range(ITERS):
        image = operate()
        residual = res[place_of(0, 0)]
        stage = k + 1
        dots[stage, me, 0:1, :] = jnp.sum(residual * residual, axis=0, keepdims=True)
        dots[stage, me, 1:2, :] = jnp.sum(residual * image, axis=0, keepdims=True)
        share(stage)
        if k < ITERS - 1:
            tiles[stage + 1] = image
            halo_copies = around(stage + 1)
            begin(halo_copies)
            copies.append(halo_copies)
        sums = totals(stage)
        norm, inner = sums[0:1, :], sums[1:2, :]
        if k == 0:
            size = norm / inner
            direction = residual
        else:
            ratio = norm / norm_before
            size = norm / (inner - ratio * norm / size_before)
            direction = residual + ratio * direction
        step = step + size * direction
        norm_before, size_before = norm, size
        if k < ITERS - 1:
            arrive(halo_copies)
            halo[stage + 1, place_of(0, 0)] = image
            flow = halo[stage + 1]
            if k > 0:
                flow = flow + ratio * img[...]
            img[...] = flow
            res[...] = res[...] - size * flow

    result = tiles[0] + step
    for j in range(COMPS):
        out_field[j, 0] = result[j * rows : (j + 1) * rows]
    for listed in copies:
        sent(listed)
    for stage in range(ITERS + 1):
        shared(dot_send, stage)
    store.wait()


def body(slabs, planes, images, shifts, initial_displacement):
    _, zs, ys, xs = images.shape
    layers, rows, across = shifts.shape[1:]
    elem = xs // across
    assert layers == 1 and zs == elem and elem == TILE and 4 * rows == TILE
    devices = slabs * planes
    parts, arrays = matrices(elem, rows, across)
    total = parts[-1][0] + parts[-1][1] + TILE
    vmem = pl.BlockSpec(memory_space=pltpu.VMEM)
    hbm = pl.BlockSpec(memory_space=pl.ANY)
    stages = ITERS + 1
    dma = pltpu.SemaphoreType.DMA

    def held(*shape):
        return pltpu.VMEM(shape, F32)

    return pl.pallas_call(
        functools.partial(kernel, slabs, planes, parts),
        out_shape=(
            jax.ShapeDtypeStruct(initial_displacement.shape, F32),
            jax.ShapeDtypeStruct(images.shape[1:], F32),
        ),
        in_specs=[hbm] + [vmem] * (2 + len(arrays)),
        out_specs=(vmem, hbm),
        scratch_shapes=[
            held(zs + 4, ys + 2 * TILE, xs),
            held(zs + 2, ys + 2 * TILE, xs),
            held(2, 3 * zs, xs),
            held(2, 3 * zs, xs),
            held(4, zs, xs),
            held(stages, TILE, across),
            held(stages, 9, TILE, across),
            held(stages, devices, 2, across),
            held(COMPS, zs, ys, xs),
            held(zs, ys, xs),
            held(4 * TILE, xs),
            held(3, TILE, xs),
            held(len(PAIRS) * 3 * ys, xs),
            held(COMPS * 2 * ys, xs),
            held(total, 2 * across),
            held(total, 2 * across),
            held(COMPS * 9 * TILE, 2 * across),
            held(9, TILE, across),
            held(9, TILE, across),
            dma((2,)),
            dma,
            dma((2, 2)),
            dma((2, 2)),
            dma((2,)),
            dma((2,)),
            dma((4,)),
            dma((4,)),
            dma((stages, 8)),
            dma((stages, 8)),
            dma((stages,)),
            dma((stages,)),
            dma((3,)),
            dma((3,)),
        ],
        compiler_params=pltpu.CompilerParams(
            collective_id=0, has_side_effects=True, vmem_limit_bytes=40 * 1024 * 1024
        ),
        name="gauss_newton_step",
    )(images, shifts, initial_displacement, *[jnp.asarray(a) for a in arrays])


def solution(mesh):
    in_specs = (
        P(None, "slab", "plane", None),
        P(None, "slab", "plane", None),
        P(None, "slab", "plane", None),
    )
    out_specs = (P(None, "slab", "plane", None), P("slab", "plane", None))
    run = functools.partial(body, mesh.shape["slab"], mesh.shape["plane"])
    return jax.shard_map(run, mesh=mesh, in_specs=in_specs, out_specs=out_specs, check_vma=False)
```

time: 964 us -> 76.5 us (0.08)
  blocking collectives: 499 us -> 0 us
  other arithmetic: 139 us -> 0 us
  starting transfers between devices: 136 us -> 0 us
  local copies, waits for them, and re-layouts: 140 us -> 11.3 us
  Pallas kernels: 0 us -> 64.1 us
  waiting for transfers between devices: 24.5 us -> 0 us
  between operations: 18.8 us -> 0.66 us
    psum x12 -> x0, blocking collectives: 499 us -> none  [the longest x6 248 us: residual_norm(): return lax.psum(jnp.sum(residual * residual * counted), ('slab', 'plane'))]
    ppermute x46 -> x0, starting transfers between devices: 136 us -> none  [the longest x16 58 us: extended(): lax.ppermute(lax.slice_in_dim(block, block.shape[dim] - width, None, axis...]
    pallas_call x0 -> x1, Pallas kernels: none -> 64.1 us  [body(): pl.pallas_call(functools.partial(kernel, slabs, planes, parts), out_shape...]
    sub x2 -> x0, other arithmetic: 59.7 us -> none  [the longest x1 58.9 us: body(): mismatch = images[0] - warped - jnp.sum(grads * moved, 0)]
    eq x54 -> x0, local copies, waits for them, and re-layouts: 40.7 us -> none  [warp_image(): result = jnp.where(codes == candidate, piece, result)]
    ppermute x46 -> x0, waiting for transfers between devices: 24.5 us -> none  [the longest x16 10 us: extended(): lax.ppermute(lax.slice_in_dim(block, 0, width, axis=dim), axis, backward)]
    reduce_sum x40 -> x0, other arithmetic: 23 us -> none  [the longest x7 9.63 us: collapse_width(): upper = jnp.sum(blocks * weights, -1)]
    concatenate x22 -> x0, other arithmetic: 20.9 us -> none  [extended(): block = jnp.concatenate([low, block, high], axis=dim)]
  transfers between devices with their start and end apart: 46 -> 0, of which waited for: 18 -> 0; matrix products, arithmetic and copies ran while one was open for 22% -> 0% of each run, Pallas kernels for 0% -> 0%
where the time goes in v1:
time: 76.5 us; the launch traced here: 76 us
  Pallas kernels  64.1 us (84%)
  local copies, waits for them, and re-layouts  11.3 us (15%)
    pallas_call x1, Pallas kernels, body(): pl.pallas_call(functools.partial(kernel, slabs, planes, parts), out_shape...  64.1 us
    unnamed x24, local copies, waits for them, and re-layouts  11.3 us

profile of v1, /device:TPU:0, one launch (start us, length us, event | category | flops | bytes accessed | tf_op | source)
XLA Modules:
  0.0 76.0 jit_solution(16911680792498997530)
XLA Ops:
  0.6 0.0 copy-start.8
  0.6 0.7 copy-done.8
  1.3 0.0 copy-start
  1.3 1.2 %copy-done = f32[2,8,16,1024]{3,2,1,0:T(8,128)S(1)} copy-done((f32[2,8,16,1024]{3,2,1,0:T(8,128)S(1)}, f32[2,8,16,1024]{3,2,1,0:T(8,128)}, u32[]{:S(2)}) %copy-start) | copy-done | bytes 1048600
  2.6 0.0 copy-start.1
  2.6 1.0 %copy-done.1 = bf16[1024,256]{1,0:T(8,128)(2,1)S(1)} copy-done((bf16[1024,256]{1,0:T(8,128)(2,1)S(1)}, bf16[1024,256]{1,0:T(8,128)(2,1)}, u32[]{:S(2)}) %copy-start.1) | copy-done | bytes 524312
  3.6 0.0 copy-start.2
  3.6 0.9 %copy-done.2 = bf16[128,1024]{1,0:T(8,128)(2,1)S(1)} copy-done((bf16[128,1024]{1,0:T(8,128)(2,1)S(1)}, bf16[128,1024]{1,0:T(8,128)(2,1)}, u32[]{:S(2)}) %copy-start.2) | copy-done | bytes 262168
  4.5 0.0 copy-start.3
  4.6 0.9 %copy-done.3 = bf16[128,1024]{1,0:T(8,128)(2,1)S(1)} copy-done((bf16[128,1024]{1,0:T(8,128)(2,1)S(1)}, bf16[128,1024]{1,0:T(8,128)(2,1)}, u32[]{:S(2)}) %copy-start.3) | copy-done | bytes 262168
  5.5 0.0 copy-start.4
  5.5 0.9 %copy-done.4 = bf16[1024,128]{1,0:T(8,128)(2,1)S(1)} copy-done((bf16[1024,128]{1,0:T(8,128)(2,1)S(1)}, bf16[1024,128]{1,0:T(8,128)(2,1)}, u32[]{:S(2)}) %copy-start.4) | copy-done | bytes 262168
  6.4 0.0 copy-start.5
  6.5 0.9 %copy-done.5 = bf16[216,288]{1,0:T(8,128)(2,1)S(1)} copy-done((bf16[216,288]{1,0:T(8,128)(2,1)S(1)}, bf16[216,288]{1,0:T(8,128)(2,1)}, u32[]{:S(2)}) %copy-start.5) | copy-done | bytes 124440
  7.4 0.0 copy-start.6
  7.4 0.9 %copy-done.6 = bf16[216,144]{1,0:T(8,128)(2,1)S(1)} copy-done((bf16[216,144]{1,0:T(8,128)(2,1)S(1)}, bf16[216,144]{1,0:T(8,128)(2,1)}, u32[]{:S(2)}) %copy-start.6) | copy-done | bytes 62232
  8.3 0.0 copy-start.7
  8.3 0.9 %copy-done.7 = bf16[144,288]{1,0:T(8,128)(2,1)S(1)} copy-done((bf16[144,288]{1,0:T(8,128)(2,1)S(1)}, bf16[144,288]{1,0:T(8,128)(2,1)}, u32[]{:S(2)}) %copy-start.7) | copy-done | bytes 82968
  9.2 0.0 copy-start.9
  9.2 0.7 copy-done.9
  9.8 0.0 copy-start.10
  9.8 0.7 copy-done.10
  10.5 64.1 %gauss_newton_step.1 = (f32[3,1,2,128]{3,2,1,0:T(2,128)S(1)}, f32[8,16,1024]{2,1,0:T(8,128)S(1)}) custom-call(f32[2,8,16,1024]{3,2,1,0:T(8,128)S(1)} %copy-done, s32[3,1,2,128]{3,2,1,0:T(2,128)S(1)} %copy-done.9, f32[3,1,2,128]{3,2,1,0:T(2,128)S(1)} %copy-done.10, bf16[1024,256]{1,0:T(8,128)(2,1)S(1)} %copy-done.1, bf16[1024,128]{1,0:T(8,128)(2,1)S(1)} %copy-done.4, ...), custom_call_target="tpu_custom_call" | custom-call | tf_op jit(solution)/shard_map/gauss_newton_step/pallas_call | solution.py:610
  74.7 0.6 copy.15
  75.2 0.8 %copy.16 = f32[8,16,1024]{2,1,0:T(8,128)} copy(f32[8,16,1024]{2,1,0:T(8,128)S(1)} %get-tuple-element.5) | data formatting | bytes 1048576
Async XLA Ops:
  0.6 0.7 copy-start.8
  1.3 1.2 %copy-start = (f32[2,8,16,1024]{3,2,1,0:T(8,128)S(1)}, f32[2,8,16,1024]{3,2,1,0:T(8,128)}, u32[]{:S(2)}) copy-start(f32[2,8,16,1024]{3,2,1,0:T(8,128)} %images.1) | copy-start | bytes 3145732
  2.6 1.0 %copy-start.1 = (bf16[1024,256]{1,0:T(8,128)(2,1)S(1)}, bf16[1024,256]{1,0:T(8,128)(2,1)}, u32[]{:S(2)}) copy-start(bf16[1024,256]{1,0:T(8,128)(2,1)} %constant.16.clone.w_stencil) | copy-start | bytes 1572868
  3.6 0.9 %copy-start.2 = (bf16[128,1024]{1,0:T(8,128)(2,1)S(1)}, bf16[128,1024]{1,0:T(8,128)(2,1)}, u32[]{:S(2)}) copy-start(bf16[128,1024]{1,0:T(8,128)(2,1)} %constant.19.clone.w_spread) | copy-start | bytes 786436
  4.5 0.9 %copy-start.3 = (bf16[128,1024]{1,0:T(8,128)(2,1)S(1)}, bf16[128,1024]{1,0:T(8,128)(2,1)}, u32[]{:S(2)}) copy-start(bf16[128,1024]{1,0:T(8,128)(2,1)} %constant.18.clone.w_nodes) | copy-start | bytes 786436
  5.5 0.9 %copy-start.4 = (bf16[1024,128]{1,0:T(8,128)(2,1)S(1)}, bf16[1024,128]{1,0:T(8,128)(2,1)}, u32[]{:S(2)}) copy-start(bf16[1024,128]{1,0:T(8,128)(2,1)} %constant.17.clone.w_hats) | copy-start | bytes 786436
  6.4 0.9 %copy-start.5 = (bf16[216,288]{1,0:T(8,128)(2,1)S(1)}, bf16[216,288]{1,0:T(8,128)(2,1)}, u32[]{:S(2)}) copy-start(bf16[216,288]{1,0:T(8,128)(2,1)} %constant.21.clone.w_own) | copy-start | bytes 373252
  7.4 0.9 %copy-start.6 = (bf16[216,144]{1,0:T(8,128)(2,1)S(1)}, bf16[216,144]{1,0:T(8,128)(2,1)}, u32[]{:S(2)}) copy-start(bf16[216,144]{1,0:T(8,128)(2,1)} %constant.22.clone.w_came) | copy-start | bytes 186628
  8.3 0.9 %copy-start.7 = (bf16[144,288]{1,0:T(8,128)(2,1)S(1)}, bf16[144,288]{1,0:T(8,128)(2,1)}, u32[]{:S(2)}) copy-start(bf16[144,288]{1,0:T(8,128)(2,1)} %constant.20.clone.w_send) | copy-start | bytes 248836
  9.2 0.7 copy-start.9
  9.8 0.7 copy-start.10

commit v2 on v1

--- a/solution.py
+++ b/solution.py
@@ -2,7 +2,6 @@
 
 import jax
 import jax.numpy as jnp
-import ml_dtypes
 import numpy as np
 from jax import lax
 from jax.experimental import pallas as pl
@@ -72,8 +71,8 @@
             send[parts[part][0] + n, column(ij, cz, r)] = squares[cy]
             index[part][key] = parts[part][0] + n
 
-    own = np.zeros((COMPS * 9 * TILE, depth))
-    came = np.zeros((COMPS * 9 * TILE, total))
+    own = np.zeros((COMPS * 9 * TILE + TILE, depth))
+    came = np.zeros((COMPS * 9 * TILE + TILE, total))
     for i in range(COMPS):
         for dz in (-1, 0, 1):
             for dy in (-1, 0, 1):
@@ -110,7 +109,7 @@
         for cz in (0, 1):
             loads[(2 + cz) * TILE + i * rows, line_of(i, cz, last)] = w
     arrays = (stencil, hats, hats.T, spread, send, own, came, loads)
-    return parts, [np.asarray(a, dtype=ml_dtypes.bfloat16) for a in arrays]
+    return parts, [np.asarray(a, dtype=np.float32) for a in arrays]
 
 
 def split(x):
@@ -137,16 +136,16 @@
     planes,
     parts,
     images,
-    shifts,
-    start_field,
-    w_stencil,
-    w_hats,
-    w_nodes,
-    w_spread,
-    w_send,
-    w_own,
-    w_came,
-    w_loads,
+    shifts_in,
+    start_in,
+    w_stencil_in,
+    w_hats_in,
+    w_nodes_in,
+    w_spread_in,
+    w_send_in,
+    w_own_in,
+    w_came_in,
+    w_loads_in,
     out_field,
     out_mismatch,
     ref_ext,
@@ -168,7 +167,18 @@
     coefs,
     res,
     img,
+    shifts,
+    start_field,
+    w_stencil,
+    w_hats,
+    w_nodes,
+    w_spread,
+    w_send,
+    w_own,
+    w_came,
+    w_loads,
     load_sem,
+    const_sem,
     out_sem,
     face_send,
     face_recv,
@@ -184,7 +194,7 @@
     part_recv,
 ):
     _, zs, ys, xs = images.shape
-    rows, across = shifts.shape[2], shifts.shape[3]
+    rows, across = shifts_in.shape[2], shifts_in.shape[3]
     elem = xs // across
     devices = slabs * planes
     slab, plane = lax.axis_index("slab"), lax.axis_index("plane")
@@ -201,31 +211,52 @@
     def beside(dz, dy):
         return (slab + dz, plane + dy)
 
-    def other(k):
-        to = lax.rem(me + k, devices)
-        return (lax.div(to, planes), lax.rem(to, planes))
+    plane_to = [plane] + [jnp.where(plane + k < planes, plane + k, plane + k - planes) for k in range(1, planes)]
+
+    def everyone(action):
+        for to in plane_to[1:]:
+            action((slab, to))
+
+        def there(k, carry):
+            at = jnp.where(slab + k < slabs, slab + k, slab + k - slabs)
+            for to in plane_to:
+                action((at, to))
+            return carry
+
+        lax.fori_loop(1, slabs, there, 0)
 
     mine = [
         pltpu.make_async_copy(images.at[0], ref_ext.at[pl.ds(2, zs), pl.ds(TILE, ys)], load_sem.at[0]),
         pltpu.make_async_copy(images.at[1], def_ext.at[pl.ds(1, zs), pl.ds(TILE, ys)], load_sem.at[1]),
     ]
-    for copy in mine:
+    small = [
+        pltpu.make_async_copy(src, dst, const_sem.at[n])
+        for n, (src, dst) in enumerate(
+            (
+                (start_in, start_field),
+                (shifts_in, shifts),
+                (w_spread_in, w_spread),
+                (w_nodes_in, w_nodes),
+                (w_stencil_in, w_stencil),
+                (w_hats_in, w_hats),
+                (w_loads_in, w_loads),
+                (w_send_in, w_send),
+                (w_own_in, w_own),
+                (w_came_in, w_came),
+            )
+        )
+    ]
+    for copy in mine + small:
         copy.start()
     halo[...] = jnp.zeros(halo.shape, F32)
     tiles[...] = jnp.zeros(tiles.shape, F32)
     got_buf[...] = jnp.zeros(got_buf.shape, F32)
+    barrier = pltpu.get_barrier_semaphore()
+    everyone(lambda to: pl.semaphore_signal(barrier, inc=1, device_id=to, device_id_type=MESH))
+    for copy in small[:1] + mine:
+        copy.wait()
     for j in range(COMPS):
         tiles[0, j * rows : (j + 1) * rows, :] = start_field[j, 0]
-
-    barrier = pltpu.get_barrier_semaphore()
-
-    def greet(k, carry):
-        pl.semaphore_signal(barrier, inc=1, device_id=other(k), device_id_type=MESH)
-        return carry
-
-    lax.fori_loop(1, devices, greet, 0)
-    for copy in mine:
-        copy.wait()
 
     for side, (far, near) in enumerate(((1, 0), (ys - 2, ys - 1))):
         pack[side, 0:zs, :] = ref_ext[2 : 2 + zs, TILE + far, :]
@@ -286,12 +317,8 @@
             pl.when(present(dz, dy))(copy.wait_send)
 
     def share(stage):
-        def one(k, carry):
-            slot = dots.at[stage, me]
-            remote(slot, slot, dot_send.at[stage], dot_recv.at[stage], other(k)).start()
-            return carry
-
-        lax.fori_loop(1, devices, one, 0)
+        slot = dots.at[stage, me]
+        everyone(lambda to: remote(slot, slot, dot_send.at[stage], dot_recv.at[stage], to).start())
 
     def shared(sem, stage):
         some = dots.at[stage, pl.ds(0, devices - 1)]
@@ -304,20 +331,23 @@
 
     image_copies = faces()
     start_copies = around(0)
-    begin(image_copies)
+    begin(image_copies[:4])
     begin(start_copies)
+    begin(image_copies[4:])
+    for copy in small[1:]:
+        copy.wait()
 
     codes = jnp.concatenate([shifts[j, 0] for j in range(COMPS)], axis=0).astype(F32).astype(BF16)
-    wide = dot(codes, w_spread[...])
+    wide = dot(codes, w_spread[...].astype(BF16))
     for n, dx in enumerate((-1, 0, 1)):
         moves[n, 0 : COMPS * rows, :] = pltpu.roll(wide, dx % xs, 1) if dx else wide
 
     arrive(start_copies)
     halo[0, place_of(0, 0)] = tiles[0]
     corner = jnp.concatenate([halo[0, place_of(dz, dy)] for dz in (0, 1) for dy in (0, 1)], axis=0)
-    nodes_x[...] = dot_left(corner, w_nodes[...])
-
-    arrive(image_copies)
+    nodes_x[...] = dot_left(corner, w_nodes[...].astype(BF16))
+
+    arrive(image_copies[4:6])
 
     def clear(dz, dy, *views):
         def run():
@@ -326,12 +356,8 @@
 
         pl.when(jnp.logical_not(present(dz, dy)))(run)
 
-    clear(-1, 0, (ref_ext, (slice(0, 2),)), (def_ext, (slice(0, 1),)))
-    clear(1, 0, (ref_ext, (slice(2 + zs, 4 + zs),)), (def_ext, (slice(1 + zs, 2 + zs),)))
     for n, d in enumerate((1, -1)):
         clear(0, d, (got_rows, (n,)))
-    for n, (dz, dy) in enumerate(((1, 1), (1, -1), (-1, 1), (-1, -1))):
-        clear(dz, dy, (got_diag, (n,)))
     top = TILE + ys
     ref_ext[2 : 2 + zs, top, :] = got_rows[0, zs : 2 * zs, :]
     ref_ext[2 : 2 + zs, top + 1, :] = got_rows[0, 0:zs, :]
@@ -339,11 +365,6 @@
     ref_ext[2 : 2 + zs, TILE - 2, :] = got_rows[1, 0:zs, :]
     ref_ext[2 : 2 + zs, TILE - 1, :] = got_rows[1, zs : 2 * zs, :]
     def_ext[1 : 1 + zs, TILE - 1, :] = got_rows[1, 2 * zs :, :]
-    def_ext[1 + zs, top : top + 1, :] = got_diag[0, 0:1, :]
-    def_ext[1 + zs, TILE - 1 : TILE, :] = got_diag[1, 0:1, :]
-    def_ext[0, top : top + 1, :] = got_diag[2, zs - 1 : zs, :]
-    def_ext[0, TILE - 1 : TILE, :] = got_diag[3, zs - 1 : zs, :]
-
     lane = lax.broadcasted_iota(jnp.int32, (TILE, xs), 1)
     up = lax.broadcasted_iota(jnp.int32, (TILE, xs), 0).astype(F32) / elem
 
@@ -407,7 +428,18 @@
             mis[z, r * elem : (r + 1) * elem, :] = total
         return energy
 
-    energy = lax.fori_loop(0, zs, voxels, jnp.zeros((TILE, xs), F32))
+    energy = lax.fori_loop(2, zs - 2, voxels, jnp.zeros((TILE, xs), F32))
+    arrive(image_copies[:4] + image_copies[6:])
+    clear(-1, 0, (ref_ext, (slice(0, 2),)), (def_ext, (slice(0, 1),)))
+    clear(1, 0, (ref_ext, (slice(2 + zs, 4 + zs),)), (def_ext, (slice(1 + zs, 2 + zs),)))
+    for n, (dz, dy) in enumerate(((1, 1), (1, -1), (-1, 1), (-1, -1))):
+        clear(dz, dy, (got_diag, (n,)))
+    def_ext[1 + zs, top : top + 1, :] = got_diag[0, 0:1, :]
+    def_ext[1 + zs, TILE - 1 : TILE, :] = got_diag[1, 0:1, :]
+    def_ext[0, top : top + 1, :] = got_diag[2, zs - 1 : zs, :]
+    def_ext[0, TILE - 1 : TILE, :] = got_diag[3, zs - 1 : zs, :]
+    energy = lax.fori_loop(0, 2, voxels, energy)
+    energy = lax.fori_loop(zs - 2, zs, voxels, energy)
     store = pltpu.make_async_copy(mis, out_mismatch, out_sem)
     store.start()
     energy = jnp.sum(energy, axis=0, keepdims=True)
@@ -457,9 +489,9 @@
         return carry
 
     lax.fori_loop(0, rows * lines, gather, 0)
-    summed = dot_left(moments[...], w_stencil[...])
-    load_tiles = dot_right(w_loads[...], dot_left(loads[...], w_hats[...]))
-    send_buf[...] = dot_right(w_send[...], summed)
+    summed = dot_left(moments[...], w_stencil[...].astype(BF16))
+    load_tiles = dot_right(w_loads[...].astype(BF16), dot_left(loads[...], w_hats[...].astype(BF16)))
+    send_buf[...] = dot_right(w_send[...].astype(BF16), summed)
     for (start, used), n in zip(parts, (1, 2, 3)):
         send_buf[start + used : start + used + TILE, :across] = load_tiles[n * TILE : (n + 1) * TILE]
     part_copies = []
@@ -469,7 +501,7 @@
             (to, remote(send_buf.at[at], got_buf.at[at], part_send.at[n], part_recv.at[n], beside(*to)))
         )
     begin(part_copies)
-    coefs[...] = dot_right(w_own[...], summed)
+    coefs[...] = dot_right(w_own[...].astype(BF16), summed)
 
     node_lane = lax.broadcasted_iota(jnp.int32, (TILE, across), 1)
     sub = lax.broadcasted_iota(jnp.int32, (TILE, across), 0)
@@ -504,7 +536,7 @@
     rhs_copies = around(1)
     begin(rhs_copies)
 
-    coefs[...] = coefs[...] + dot_right(w_came[...], got_buf[...])
+    coefs[...] = coefs[...] + dot_right(w_came[...].astype(BF16), got_buf[...])
     for i in range(COMPS):
         same = jnp.where(group == i, 1.0, 0.0) * penalty
 
@@ -600,7 +632,7 @@
     parts, arrays = matrices(elem, rows, across)
     total = parts[-1][0] + parts[-1][1] + TILE
     vmem = pl.BlockSpec(memory_space=pltpu.VMEM)
-    hbm = pl.BlockSpec(memory_space=pl.ANY)
+    hbm = pl.BlockSpec(memory_space=pltpu.HBM)
     stages = ITERS + 1
     dma = pltpu.SemaphoreType.DMA
 
@@ -613,7 +645,7 @@
             jax.ShapeDtypeStruct(initial_displacement.shape, F32),
             jax.ShapeDtypeStruct(images.shape[1:], F32),
         ),
-        in_specs=[hbm] + [vmem] * (2 + len(arrays)),
+        in_specs=[hbm] * (3 + len(arrays)),
         out_specs=(vmem, hbm),
         scratch_shapes=[
             held(zs + 4, ys + 2 * TILE, xs),
@@ -632,10 +664,14 @@
             held(COMPS * 2 * ys, xs),
             held(total, 2 * across),
             held(total, 2 * across),
-            held(COMPS * 9 * TILE, 2 * across),
+            held(COMPS * 9 * TILE + TILE, 2 * across),
             held(9, TILE, across),
             held(9, TILE, across),
+            pltpu.VMEM(shifts.shape, jnp.int32),
+            held(*initial_displacement.shape),
+            *[held(*a.shape) for a in arrays],
             dma((2,)),
+            dma((2 + len(arrays),)),
             dma,
             dma((2, 2)),
             dma((2, 2)),
@@ -651,7 +687,7 @@
             dma((3,)),
         ],
         compiler_params=pltpu.CompilerParams(
-            collective_id=0, has_side_effects=True, vmem_limit_bytes=40 * 1024 * 1024
+            collective_id=0, has_side_effects=True, vmem_limit_bytes=56 * 1024 * 1024
         ),
         name="gauss_newton_step",
     )(images, shifts, initial_displacement, *[jnp.asarray(a) for a in arrays])

time: 76.5 us -> 66.6 us (0.87)
  local copies, waits for them, and re-layouts: 11.3 us -> 3.14 us
  Pallas kernels: 64.1 us -> 62.6 us
    unnamed x24 -> x4, local copies, waits for them, and re-layouts: 11.3 us -> 3.14 us
    pallas_call x1, Pallas kernels: 64.1 us -> 62.6 us  [body(): pl.pallas_call(functools.partial(kernel, slabs, planes, parts), out_shape...]
where the time goes in v2:
time: 66.6 us; the launch traced here: 66.4 us
  Pallas kernels  62.6 us (94%)
  local copies, waits for them, and re-layouts  3.14 us (5%)
    pallas_call x1, Pallas kernels, body(): pl.pallas_call(functools.partial(kernel, slabs, planes, parts), out_shape...  62.6 us
    unnamed x4, local copies, waits for them, and re-layouts  3.14 us

profile of v2, /device:TPU:0, one launch (start us, length us, event | category | flops | bytes accessed | tf_op | source)
XLA Modules:
  0.0 66.4 jit_solution(16386239271065597418)
XLA Ops:
  0.6 62.6 %gauss_newton_step.1 = (f32[3,1,2,128]{3,2,1,0:T(2,128)}, f32[8,16,1024]{2,1,0:T(8,128)}) custom-call(f32[2,8,16,1024]{3,2,1,0:T(8,128)} %images.1, s32[3,1,2,128]{3,2,1,0:T(2,128)} %shifts_in.1, f32[3,1,2,128]{3,2,1,0:T(2,128)} %start_in.1, f32[1024,256]{1,0:T(8,128)} %constant.16.clone.w_stencil_in, f32[1024,128]{1,0:T(8,128)} %constant.17.clone.w_hats_in, ...), custom_call_target="tpu_custom_call" | custom-call | tf_op jit(solution)/shard_map/gauss_newton_step/pallas_call | solution.py:642
  63.3 0.0 copy-start
  63.3 0.7 %copy-done = f32[3,1,2,128]{3,2,1,0:T(2,128)S(1)} copy-done((f32[3,1,2,128]{3,2,1,0:T(2,128)S(1)}, f32[3,1,2,128]{3,2,1,0:T(2,128)}, u32[]{:S(2)}) %copy-start) | copy-done | bytes 3096
  64.0 0.6 copy.15
  64.5 1.9 %copy.16 = f32[8,16,1024]{2,1,0:T(8,128)} copy(f32[8,16,1024]{2,1,0:T(8,128)} %get-tuple-element.5) | data formatting | bytes 1048576
Async XLA Ops:
  63.3 0.7 %copy-start = (f32[3,1,2,128]{3,2,1,0:T(2,128)S(1)}, f32[3,1,2,128]{3,2,1,0:T(2,128)}, u32[]{:S(2)}) copy-start(f32[3,1,2,128]{3,2,1,0:T(2,128)} %get-tuple-element.4) | copy-start | bytes 9220

commit v3 on v2

--- a/solution.py
+++ b/solution.py
@@ -9,6 +9,8 @@
 from jax.sharding import PartitionSpec as P
 
 ITERS = 6
+BLOCK = ITERS // 2
+SPREAD = 128.0
 reg_weight = 4.0
 
 MESH = pl.DeviceIdType.MESH
@@ -129,6 +131,81 @@
 def dot_right(exact, x):
     high, low = split(x)
     return dot(exact, high) + dot(exact, low)
+
+
+def times(a, b):
+    if isinstance(a, float) and a == 0.0 or isinstance(b, float) and b == 0.0:
+        return 0.0
+    if isinstance(a, float) and a == 1.0:
+        return b
+    if isinstance(b, float) and b == 1.0:
+        return a
+    return a * b
+
+
+def total(a, b):
+    if isinstance(a, float) and a == 0.0:
+        return b
+    if isinstance(b, float) and b == 0.0:
+        return a
+    return a + b
+
+
+def lifted(poly):
+    return [0.0] + list(poly)
+
+
+def plus(a, b, factor):
+    out = list(a) + [0.0] * (len(b) - len(a))
+    for k, value in enumerate(b):
+        out[k] = total(out[k], times(factor, value))
+    return out
+
+
+def product(a, b):
+    out = [0.0] * (len(a) + len(b) - 1)
+    for i, x in enumerate(a):
+        for j, y in enumerate(b):
+            out[i + j] = total(out[i + j], times(x, y))
+    return out
+
+
+def combine(poly, values):
+    out = 0.0
+    for k, value in enumerate(poly):
+        if not (isinstance(value, float) and value == 0.0):
+            out = total(out, times(value, values[k]))
+    return out
+
+
+def inner(x, y, moments):
+    out = combine(product(x[0], y[0]), moments[0])
+    mixed = plus(product(x[0], y[1]), product(x[1], y[0]), 1.0)
+    out = total(out, combine(mixed, moments[1]))
+    return total(out, combine(product(x[1], y[1]), moments[2]))
+
+
+def conjugate(residual, direction, moments, shift, steps, go_on):
+    moved = ([0.0], [0.0])
+    norm = inner(residual, residual, moments)
+    turns = 0.0
+    past = None
+    for k in range(steps):
+        image = tuple(plus(lifted(d), d, shift) for d in direction)
+        bend = inner(direction, image, moments)
+        size = norm / bend
+        moved = tuple(plus(m, d, size) for m, d in zip(moved, direction))
+        if k == steps - 1 and not go_on:
+            break
+        before, old = residual, direction
+        residual = tuple(plus(r, i, -size) for r, i in zip(residual, image))
+        fresh = inner(residual, residual, moments)
+        ratio = fresh / norm
+        direction = tuple(plus(r, d, ratio) for r, d in zip(residual, direction))
+        turns = total(turns, (bend / norm) * (1.0 / steps))
+        norm = fresh
+        past = (old[1], before[1], size, ratio, turns)
+    return moved, residual, direction, past
 
 
 def kernel(
@@ -166,7 +243,6 @@
     got_buf,
     coefs,
     res,
-    img,
     shifts,
     start_field,
     w_stencil,
@@ -552,15 +628,14 @@
 
     arrive(rhs_copies)
     halo[1, place_of(0, 0)] = rhs
-    res[...] = halo[1]
-    img[...] = jnp.zeros(img.shape, F32)
-
-    def operate():
+    scale = 1.0 / (penalty * SPREAD)
+
+    def operate(get, shift):
         out = [None] * COMPS
         back = [None] * COMPS
         for dz in (-1, 0, 1):
             for dy in (-1, 0, 1):
-                v = neighbour(lambda place: res[place], dz, dy)
+                v = neighbour(get, dz, dy)
                 ahead = pltpu.roll(v, across - 1, 1)
                 for i in range(COMPS):
                     at = pl.ds((i * 9 + place_of(dz, dy)) * TILE, TILE)
@@ -575,50 +650,100 @@
             value = value + pltpu.roll(value, TILE // 2, 0)
             value = value + pltpu.roll(value, rows, 0)
             image = jnp.where(group == i, value, image)
-        return image
-
-    direction = jnp.zeros((TILE, across), F32)
-    step = jnp.zeros((TILE, across), F32)
-    norm_before = size_before = None
+        return image * scale - shift * get(place_of(0, 0))
+
     copies = [image_copies, start_copies, part_copies, rhs_copies]
-    for k in range(ITERS):
-        image = operate()
-        residual = res[place_of(0, 0)]
-        stage = k + 1
-        dots[stage, me, 0:1, :] = jnp.sum(residual * residual, axis=0, keepdims=True)
-        dots[stage, me, 1:2, :] = jnp.sum(residual * image, axis=0, keepdims=True)
+
+    def spread(stage, image):
+        tiles[stage] = image
+        listed = around(stage)
+        begin(listed)
+        copies.append(listed)
+        return listed
+
+    def landed(stage, listed, image):
+        arrive(listed)
+        halo[stage, place_of(0, 0)] = image
+
+    def publish(stage, products):
+        lines = [jnp.sum(p, axis=0, keepdims=True) for p in products]
+        fill = -len(lines) % TILE
+        lines += [jnp.zeros((1, across), F32)] * fill
+        stacked = jnp.concatenate(lines, axis=0)
+        column = jnp.sum(stacked, axis=1, keepdims=True)
+        at = lax.broadcasted_iota(jnp.int32, stacked.shape, 0) == lax.broadcasted_iota(jnp.int32, stacked.shape, 1)
+        dots[stage, me] = jnp.zeros(dots.shape[2:], F32)
+        dots[stage, me, 0:1, :] = jnp.sum(jnp.where(at, column, 0.0), axis=0, keepdims=True)
         share(stage)
-        if k < ITERS - 1:
-            tiles[stage + 1] = image
-            halo_copies = around(stage + 1)
-            begin(halo_copies)
-            copies.append(halo_copies)
-        sums = totals(stage)
-        norm, inner = sums[0:1, :], sums[1:2, :]
-        if k == 0:
-            size = norm / inner
-            direction = residual
-        else:
-            ratio = norm / norm_before
-            size = norm / (inner - ratio * norm / size_before)
-            direction = residual + ratio * direction
-        step = step + size * direction
-        norm_before, size_before = norm, size
-        if k < ITERS - 1:
-            arrive(halo_copies)
-            halo[stage + 1, place_of(0, 0)] = image
-            flow = halo[stage + 1]
-            if k > 0:
-                flow = flow + ratio * img[...]
-            img[...] = flow
-            res[...] = res[...] - size * flow
+
+    def gathered(stage, count):
+        shared(dot_recv, stage)
+        row = jnp.sum(dots[stage], axis=0)[0:1, :]
+        at = lax.broadcasted_iota(jnp.int32, row.shape, 1)
+        return [jnp.sum(jnp.where(at == k, row, 0.0), axis=1, keepdims=True) for k in range(count)]
+
+    def on(stage):
+        return lambda place: halo[stage, place]
+
+    shift = 0.25
+    basis = [rhs]
+    for k in range(BLOCK):
+        image = operate(on(k + 1), shift)
+        basis.append(image)
+        if k < BLOCK - 1:
+            landed(k + 2, spread(k + 2, image), image)
+    count = 2 * BLOCK + 1
+    publish(1, [basis[k // 2] * basis[(k + 1) // 2] for k in range(count)])
+    listed = spread(BLOCK + 1, basis[BLOCK])
+    landed(BLOCK + 1, listed, basis[BLOCK])
+    basis.append(operate(on(BLOCK + 1), shift))
+    first = gathered(1, count)
+    moved, residual, direction, past = conjugate(
+        ([0.0], [1.0]), ([0.0], [1.0]), (None, None, first), shift, BLOCK, True
+    )
+    step = combine(moved[1], basis)
+    start_poly, before, size, ratio, turns = past
+    for place in range(9):
+        res[place] = combine(residual[1], [halo[k + 1, place] for k in range(BLOCK + 1)])
+
+    later = turns
+    chain = [res[place_of(0, 0)]]
+    chain.append(operate(lambda place: res[place], later))
+    listed = spread(BLOCK + 2, chain[1])
+    lift = shift - later
+    powers = [start_poly]
+    for k in range(BLOCK - 1):
+        powers.append(plus(lifted(powers[-1]), powers[-1], lift))
+    olds = [combine(p, basis) for p in powers]
+    twice = before
+    for k in range(BLOCK - 1):
+        twice = plus(lifted(twice), twice, lift)
+    last = combine(twice, basis)
+    pulls = [chain[0] + ratio * olds[0], chain[1] + ratio * olds[1]]
+    landed(BLOCK + 2, listed, chain[1])
+    chain.append(operate(on(BLOCK + 2), later))
+    listed = spread(BLOCK + 3, chain[2])
+    pulls.append(chain[2] + ratio * olds[2])
+    old = (last - chain[2]) / size - later * olds[2]
+    landed(BLOCK + 3, listed, chain[2])
+    pulls.append(operate(on(BLOCK + 3), later) + ratio * old)
+    count = 2 * BLOCK
+    products = [pulls[k // 2] * pulls[(k + 1) // 2] for k in range(count)]
+    products += [pulls[(k + 1) // 2] * chain[k // 2] for k in range(count - 1)]
+    products += [chain[k // 2] * chain[(k + 1) // 2] for k in range(count - 2)]
+    publish(2, products)
+    second = gathered(2, len(products))
+    seconds = (second[:count], second[count : 2 * count - 1], second[2 * count - 1 :])
+    moved, _, _, _ = conjugate(([0.0], [1.0]), ([1.0], [0.0]), seconds, later, BLOCK, False)
+    step = step + combine(moved[0], pulls) + combine(moved[1], chain)
+    step = step * scale
 
     result = tiles[0] + step
     for j in range(COMPS):
         out_field[j, 0] = result[j * rows : (j + 1) * rows]
     for listed in copies:
         sent(listed)
-    for stage in range(ITERS + 1):
+    for stage in range(3):
         shared(dot_send, stage)
     store.wait()
 
@@ -655,7 +780,7 @@
             held(4, zs, xs),
             held(stages, TILE, across),
             held(stages, 9, TILE, across),
-            held(stages, devices, 2, across),
+            held(3, devices, 2, across),
             held(COMPS, zs, ys, xs),
             held(zs, ys, xs),
             held(4 * TILE, xs),
@@ -665,7 +790,6 @@
             held(total, 2 * across),
             held(total, 2 * across),
             held(COMPS * 9 * TILE + TILE, 2 * across),
-            held(9, TILE, across),
             held(9, TILE, across),
             pltpu.VMEM(shifts.shape, jnp.int32),
             held(*initial_displacement.shape),
@@ -681,8 +805,8 @@
             dma((4,)),
             dma((stages, 8)),
             dma((stages, 8)),
-            dma((stages,)),
-            dma((stages,)),
+            dma((3,)),
+            dma((3,)),
             dma((3,)),
             dma((3,)),
         ],

time: 66.6 us -> 60.6 us (0.910)
  Pallas kernels: 62.6 us -> 56.6 us
    pallas_call x1, Pallas kernels: 62.6 us -> 56.6 us  [body(): pl.pallas_call(functools.partial(kernel, slabs, planes, parts), out_shape...]
where the time goes in v3:
time: 60.6 us; the launch traced here: 60.4 us
  Pallas kernels  56.6 us (93%)
  local copies, waits for them, and re-layouts  3.14 us (5%)
  between operations  0.65 us (1%)
    pallas_call x1, Pallas kernels, body(): pl.pallas_call(functools.partial(kernel, slabs, planes, parts), out_shape...  56.6 us
    unnamed x4, local copies, waits for them, and re-layouts  3.14 us

profile of v3, /device:TPU:0, one launch (start us, length us, event | category | flops | bytes accessed | tf_op | source)
XLA Modules:
  0.0 60.4 jit_solution(13598623819008423236)
XLA Ops:
  0.6 56.6 %gauss_newton_step.1 = (f32[3,1,2,128]{3,2,1,0:T(2,128)}, f32[8,16,1024]{2,1,0:T(8,128)}) custom-call(f32[2,8,16,1024]{3,2,1,0:T(8,128)} %images.1, s32[3,1,2,128]{3,2,1,0:T(2,128)} %shifts_in.1, f32[3,1,2,128]{3,2,1,0:T(2,128)} %start_in.1, f32[1024,256]{1,0:T(8,128)} %constant.16.clone.w_stencil_in, f32[1024,128]{1,0:T(8,128)} %constant.17.clone.w_hats_in, ...), custom_call_target="tpu_custom_call" | custom-call | tf_op jit(solution)/shard_map/gauss_newton_step/pallas_call | solution.py:767
  57.3 0.0 copy-start
  57.3 0.7 %copy-done = f32[3,1,2,128]{3,2,1,0:T(2,128)S(1)} copy-done((f32[3,1,2,128]{3,2,1,0:T(2,128)S(1)}, f32[3,1,2,128]{3,2,1,0:T(2,128)}, u32[]{:S(2)}) %copy-start) | copy-done | bytes 3096
  58.0 0.6 copy.15
  58.5 1.9 %copy.16 = f32[8,16,1024]{2,1,0:T(8,128)} copy(f32[8,16,1024]{2,1,0:T(8,128)} %get-tuple-element.5) | data formatting | bytes 1048576
Async XLA Ops:
  57.3 0.7 %copy-start = (f32[3,1,2,128]{3,2,1,0:T(2,128)S(1)}, f32[3,1,2,128]{3,2,1,0:T(2,128)}, u32[]{:S(2)}) copy-start(f32[3,1,2,128]{3,2,1,0:T(2,128)} %get-tuple-element.4) | copy-start | bytes 9220

commit v4 on v3

--- a/solution.py
+++ b/solution.py
@@ -110,7 +110,17 @@
                     loads[cz * TILE + out, line_of(i, cz, r - 1)] = w
         for cz in (0, 1):
             loads[(2 + cz) * TILE + i * rows, line_of(i, cz, last)] = w
-    arrays = (stencil, hats, hats.T, spread, send, own, came, loads)
+    rise = np.zeros((COMPS, elem, height, 4 * TILE))
+    for j in range(COMPS):
+        for z in range(elem):
+            for y in range(height):
+                for dz, wz in ((0, 1 - w[z]), (1, w[z])):
+                    for up, wy in ((0, 1 - w[y % elem]), (1, w[y % elem])):
+                        line = y // elem + up
+                        at = (dz * 2 + line // rows) * TILE + j * rows + line % rows
+                        rise[j, z, y, at] += wz * wy
+    rise = rise.reshape(-1, 4 * TILE)
+    arrays = (stencil, hats, hats.T, spread, send, own, came, loads, rise)
     return parts, [np.asarray(a, dtype=np.float32) for a in arrays]
 
 
@@ -223,10 +233,12 @@
     w_own_in,
     w_came_in,
     w_loads_in,
-    out_field,
-    out_mismatch,
+    w_rise_in,
+    out_step,
+    out_model,
     ref_ext,
     def_ext,
+    def_side,
     pack,
     got_rows,
     got_diag,
@@ -234,8 +246,8 @@
     halo,
     dots,
     grads,
-    mis,
-    nodes_x,
+    model,
+    moved,
     moves,
     moments,
     loads,
@@ -253,6 +265,7 @@
     w_own,
     w_came,
     w_loads,
+    w_rise,
     load_sem,
     const_sem,
     out_sem,
@@ -319,6 +332,7 @@
                 (w_send_in, w_send),
                 (w_own_in, w_own),
                 (w_came_in, w_came),
+                (w_rise_in, w_rise),
             )
         )
     ]
@@ -421,7 +435,7 @@
     arrive(start_copies)
     halo[0, place_of(0, 0)] = tiles[0]
     corner = jnp.concatenate([halo[0, place_of(dz, dy)] for dz in (0, 1) for dy in (0, 1)], axis=0)
-    nodes_x[...] = dot_left(corner, w_nodes[...].astype(BF16))
+    moved[...] = dot_right(w_rise[...].astype(BF16), dot_left(corner, w_nodes[...].astype(BF16)))
 
     arrive(image_copies[4:6])
 
@@ -441,33 +455,59 @@
     ref_ext[2 : 2 + zs, TILE - 2, :] = got_rows[1, 0:zs, :]
     ref_ext[2 : 2 + zs, TILE - 1, :] = got_rows[1, zs : 2 * zs, :]
     def_ext[1 : 1 + zs, TILE - 1, :] = got_rows[1, 2 * zs :, :]
+    def lean(z):
+        for n, dy in enumerate((-1, 1)):
+            def_side[n, z] = def_ext[z, TILE + dy : TILE + dy + ys, :]
+
+    def lean_own(z, carry):
+        lean(z)
+        return carry
+
+    lax.fori_loop(1, zs + 1, lean_own, 0)
+
     lane = lax.broadcasted_iota(jnp.int32, (TILE, xs), 1)
-    up = lax.broadcasted_iota(jnp.int32, (TILE, xs), 0).astype(F32) / elem
 
     def along(value, d):
         rolled = pltpu.roll(value, (-d) % xs, 1)
         inside = lane < xs - d if d > 0 else lane >= -d
         return jnp.where(inside, rolled, 0.0)
 
-    def voxels(z, energy):
-        wz = z.astype(F32) / elem
+    def moved_at(j, z, r):
+        return moved[pl.ds(pl.multiple_of((j * zs + z) * ys + r * elem, elem), elem), :]
+
+    def flat(z, carry):
         for r in range(rows):
             base = TILE + r * elem
 
-            def ref(dz, dy):
-                return ref_ext[z + (2 + dz), base + dy : base + dy + elem, :]
-
-            centre = ref(0, 0)
-            g = [
-                (ref(-2, 0) - ref(2, 0) + 8.0 * (ref(1, 0) - ref(-1, 0))) * (1.0 / 12.0),
-                (ref(0, -2) - ref(0, 2) + 8.0 * (ref(0, 1) - ref(0, -1))) * (1.0 / 12.0),
-                (
-                    along(centre, -2)
-                    - along(centre, 2)
-                    + 8.0 * (along(centre, 1) - along(centre, -1))
-                )
-                * (1.0 / 12.0),
-            ]
+            def ref(dy):
+                return ref_ext[z + 2, base + dy : base + dy + elem, :]
+
+            centre = ref(0)
+            gy = (ref(-2) - ref(2) + 8.0 * (ref(1) - ref(-1))) * (1.0 / 12.0)
+            gx = along(centre, -2) - along(centre, 2) + 8.0 * (along(centre, 1) - along(centre, -1))
+            gx = gx * (1.0 / 12.0)
+            here = slice(r * elem, (r + 1) * elem)
+            grads[1, z, here, :] = gy
+            grads[2, z, here, :] = gx
+            model[z, here, :] = gy * moved_at(1, z, r) + gx * moved_at(2, z, r)
+        return carry
+
+    def deep(z, carry):
+        for r in range(rows):
+            base = TILE + r * elem
+
+            def ref(dz):
+                return ref_ext[z + (2 + dz), base : base + elem, :]
+
+            gz = (ref(-2) - ref(2) + 8.0 * (ref(1) - ref(-1))) * (1.0 / 12.0)
+            here = slice(r * elem, (r + 1) * elem)
+            grads[0, z, here, :] = gz
+            model[z, here, :] = model[z, here, :] + gz * moved_at(0, z, r)
+        return carry
+
+    def warp(z, carry):
+        for r in range(rows):
+            here = slice(r * elem, (r + 1) * elem)
             warped = None
             for n, dx in enumerate((-1, 0, 1)):
                 s = [moves[n, j * rows + r : j * rows + r + 1, :] for j in range(2)]
@@ -475,36 +515,29 @@
                 below, above = s[0] < -0.5, s[0] > 0.5
                 line = []
                 for dy in (-1, 0, 1):
-                    at = pl.ds(base + dy, elem)
-                    value = jnp.where(below, def_ext[z, at, :], def_ext[z + 1, at, :])
-                    line.append(jnp.where(above, def_ext[z + 2, at, :], value))
+
+                    def layer(dz):
+                        if dy == 0:
+                            return def_ext[z + 1 + dz, TILE + r * elem : TILE + (r + 1) * elem, :]
+                        return def_side[(dy + 1) // 2, z + 1 + dz, here, :]
+
+                    value = jnp.where(below, layer(-1), layer(0))
+                    line.append(jnp.where(above, layer(1), value))
                 value = jnp.where(s[1] < -0.5, line[0], line[1])
                 value = jnp.where(s[1] > 0.5, line[2], value)
                 if dx:
                     value = along(value, dx)
-                sx = jnp.broadcast_to(moves[1, 2 * rows + r : 2 * rows + r + 1, :], (elem, xs))
                 if warped is None:
                     warped = value
                 else:
+                    sx = jnp.broadcast_to(moves[1, 2 * rows + r : 2 * rows + r + 1, :], (elem, xs))
                     warped = jnp.where(sx > dx - 0.5, value, warped)
-            total = centre - warped
-            for j in range(COMPS):
-
-                def node(line):
-                    dy = line // rows
-                    at = j * rows + line % rows
-                    low = nodes_x[dy * TILE + at : dy * TILE + at + 1, :]
-                    high = nodes_x[(2 + dy) * TILE + at : (2 + dy) * TILE + at + 1, :]
-                    return (1.0 - wz) * low + wz * high
-
-                moved = (1.0 - up) * node(r) + up * node(r + 1)
-                total = total - g[j] * moved
-                grads[j, z, r * elem : (r + 1) * elem, :] = g[j]
-                energy = energy + g[j] * g[j]
-            mis[z, r * elem : (r + 1) * elem, :] = total
-        return energy
-
-    energy = lax.fori_loop(2, zs - 2, voxels, jnp.zeros((TILE, xs), F32))
+            model[z, here, :] = model[z, here, :] + warped
+        return carry
+
+    lax.fori_loop(0, zs, flat, 0)
+    lax.fori_loop(1, zs - 1, warp, 0)
+    lax.fori_loop(2, zs - 2, deep, 0)
     arrive(image_copies[:4] + image_copies[6:])
     clear(-1, 0, (ref_ext, (slice(0, 2),)), (def_ext, (slice(0, 1),)))
     clear(1, 0, (ref_ext, (slice(2 + zs, 4 + zs),)), (def_ext, (slice(1 + zs, 2 + zs),)))
@@ -514,19 +547,16 @@
     def_ext[1 + zs, TILE - 1 : TILE, :] = got_diag[1, 0:1, :]
     def_ext[0, top : top + 1, :] = got_diag[2, zs - 1 : zs, :]
     def_ext[0, TILE - 1 : TILE, :] = got_diag[3, zs - 1 : zs, :]
-    energy = lax.fori_loop(0, 2, voxels, energy)
-    energy = lax.fori_loop(zs - 2, zs, voxels, energy)
-    store = pltpu.make_async_copy(mis, out_mismatch, out_sem)
+    lean(0)
+    lean(zs + 1)
+    warp(0, 0)
+    warp(zs - 1, 0)
+    for z in (0, 1, zs - 2, zs - 1):
+        deep(z, 0)
+    store = pltpu.make_async_copy(model, out_model, out_sem)
     store.start()
-    energy = jnp.sum(energy, axis=0, keepdims=True)
-    dots[0, me] = jnp.zeros(dots.shape[2:], F32)
-    row = energy[:, :across]
-    for c in range(1, xs // across):
-        row = row + energy[:, c * across : (c + 1) * across]
-    dots[0, me, 0:1, :] = row
-    share(0)
-
-    width = 128
+
+    width = across
     lines = xs // width
 
     def gather(n, carry):
@@ -545,9 +575,11 @@
         for z in range(zs):
             w = z / elem
             g = [grads[j, z, ay, ax] for j in range(COMPS)]
-            q = mis[z, ay, ax]
+            q = ref_ext[2 + z, pl.ds(pl.multiple_of(TILE + r * elem, elem), elem), ax] - model[z, ay, ax]
             for ij, (i, j) in enumerate(PAIRS):
                 product = g[i] * g[j]
+                if i == j:
+                    carry = carry + product
                 for cz, weight in enumerate(((1 - w) ** 2, w * (1 - w), w * w)):
                     sums[ij][cz] = add(sums[ij][cz], weight, product)
             for i in range(COMPS):
@@ -564,7 +596,10 @@
                 loads[pl.ds(at, elem), ax] = forces[i][cz]
         return carry
 
-    lax.fori_loop(0, rows * lines, gather, 0)
+    energy = lax.fori_loop(0, rows * lines, gather, jnp.zeros((elem, width), F32))
+    dots[0, me] = jnp.zeros(dots.shape[2:], F32)
+    dots[0, me, 0:1, :] = jnp.sum(energy, axis=0, keepdims=True)
+    share(0)
     summed = dot_left(moments[...], w_stencil[...].astype(BF16))
     load_tiles = dot_right(w_loads[...].astype(BF16), dot_left(loads[...], w_hats[...].astype(BF16)))
     send_buf[...] = dot_right(w_send[...].astype(BF16), summed)
@@ -738,9 +773,8 @@
     step = step + combine(moved[0], pulls) + combine(moved[1], chain)
     step = step * scale
 
-    result = tiles[0] + step
     for j in range(COMPS):
-        out_field[j, 0] = result[j * rows : (j + 1) * rows]
+        out_step[j, 0] = step[j * rows : (j + 1) * rows]
     for listed in copies:
         sent(listed)
     for stage in range(3):
@@ -764,7 +798,7 @@
     def held(*shape):
         return pltpu.VMEM(shape, F32)
 
-    return pl.pallas_call(
+    step, model = pl.pallas_call(
         functools.partial(kernel, slabs, planes, parts),
         out_shape=(
             jax.ShapeDtypeStruct(initial_displacement.shape, F32),
@@ -775,6 +809,7 @@
         scratch_shapes=[
             held(zs + 4, ys + 2 * TILE, xs),
             held(zs + 2, ys + 2 * TILE, xs),
+            held(2, zs + 2, ys, xs),
             held(2, 3 * zs, xs),
             held(2, 3 * zs, xs),
             held(4, zs, xs),
@@ -783,7 +818,7 @@
             held(3, devices, 2, across),
             held(COMPS, zs, ys, xs),
             held(zs, ys, xs),
-            held(4 * TILE, xs),
+            held(COMPS * zs * ys, xs),
             held(3, TILE, xs),
             held(len(PAIRS) * 3 * ys, xs),
             held(COMPS * 2 * ys, xs),
@@ -815,6 +850,7 @@
         ),
         name="gauss_newton_step",
     )(images, shifts, initial_displacement, *[jnp.asarray(a) for a in arrays])
+    return initial_displacement + step, images[0] - model
 
 
 def solution(mesh):

time: 60.6 us -> 61.5 us (1.015)
  other arithmetic: 0 us -> 3.15 us
  local copies, waits for them, and re-layouts: 3.14 us -> 0.68 us
    unnamed x4, local copies, waits for them, and re-layouts: 3.14 us -> 0.68 us
    sub x0 -> x1, other arithmetic: none -> 1.9 us  [body(): return (initial_displacement + step, images[0] - model)]
    add x0 -> x1, other arithmetic: none -> 1.25 us  [body(): return (initial_displacement + step, images[0] - model)]
where the time goes in v4:
time: 61.5 us; the launch traced here: 61.3 us
  Pallas kernels  56.8 us (92%)
  other arithmetic  3.15 us (5%)
  local copies, waits for them, and re-layouts  0.68 us (1%)
  between operations  0.65 us (1%)
    pallas_call x1, Pallas kernels, body(): pl.pallas_call(functools.partial(kernel, slabs, planes, parts), out_shape...  56.8 us
    sub x1, other arithmetic, body(): return (initial_displacement + step, images[0] - model)  1.9 us
    add x1, other arithmetic, body(): return (initial_displacement + step, images[0] - model)  1.25 us

profile of v4, /device:TPU:0, one launch (start us, length us, event | category | flops | bytes accessed | tf_op | source)
XLA Modules:
  0.0 61.3 jit_solution(5072206469170312320)
XLA Ops:
  0.6 0.0 copy-start
  0.6 56.8 %gauss_newton_step.1 = (f32[3,1,2,128]{3,2,1,0:T(2,128)}, f32[8,16,1024]{2,1,0:T(8,128)}) custom-call(f32[2,8,16,1024]{3,2,1,0:T(8,128)} %images.1, s32[3,1,2,128]{3,2,1,0:T(2,128)} %shifts_in.1, f32[3,1,2,128]{3,2,1,0:T(2,128)} %start_in.1, f32[1024,256]{1,0:T(8,128)} %constant.18.clone.w_stencil_in, f32[1024,128]{1,0:T(8,128)} %constant.19.clone.w_hats_in, ...), custom_call_target="tpu_custom_call" | custom-call | tf_op jit(solution)/shard_map/gauss_newton_step/pallas_call | solution.py:801
  57.4 0.0 copy-start.1
  57.4 0.7 %copy-done.1 = f32[3,1,2,128]{3,2,1,0:T(2,128)S(1)} copy-done((f32[3,1,2,128]{3,2,1,0:T(2,128)S(1)}, f32[3,1,2,128]{3,2,1,0:T(2,128)}, u32[]{:S(2)}) %copy-start.1) | copy-done | bytes 3096
  58.1 1.3 %add.3 = f32[3,1,2,128]{3,2,1,0:T(2,128)} add(f32[3,1,2,128]{3,2,1,0:T(2,128)S(1)} %copy-done.1, f32[3,1,2,128]{3,2,1,0:T(2,128)} %get-tuple-element.4) | non-fusion elementwise | flops 768 | bytes 9216 | tf_op jit(solution)/shard_map/add | solution.py:853
  59.4 0.0 copy-done
  59.4 1.9 %bitcast_subtract_fusion = f32[8,16,1024]{2,1,0:T(8,128)} fusion(f32[8,16,1024]{2,1,0:T(8,128)} %get-tuple-element.5, f32[2,8,16,1024]{3,2,1,0:T(8,128)S(1)} %copy-done), kind=kLoop, calls=%fused_computation | loop fusion | flops 131072 | bytes 1572864 | tf_op jit(solution)/shard_map/sub | solution.py:853
Async XLA Ops:
  0.6 58.7 %copy-start = (f32[2,8,16,1024]{3,2,1,0:T(8,128)S(1)}, f32[2,8,16,1024]{3,2,1,0:T(8,128)}, u32[]{:S(2)}) copy-start(f32[2,8,16,1024]{3,2,1,0:T(8,128)} %images.1) | copy-start | bytes 3145732
  57.4 0.7 %copy-start.1 = (f32[3,1,2,128]{3,2,1,0:T(2,128)S(1)}, f32[3,1,2,128]{3,2,1,0:T(2,128)}, u32[]{:S(2)}) copy-start(f32[3,1,2,128]{3,2,1,0:T(2,128)} %start_in.1) | copy-start | bytes 9220

commit v5 on v4

--- a/solution.py
+++ b/solution.py
@@ -234,8 +234,8 @@
     w_came_in,
     w_loads_in,
     w_rise_in,
-    out_step,
-    out_model,
+    out_field,
+    out_mismatch,
     ref_ext,
     def_ext,
     def_side,
@@ -244,7 +244,8 @@
     got_diag,
     tiles,
     halo,
-    dots,
+    row_dots,
+    column_dots,
     grads,
     model,
     moved,
@@ -287,7 +288,6 @@
     elem = xs // across
     devices = slabs * planes
     slab, plane = lax.axis_index("slab"), lax.axis_index("plane")
-    me = slab * planes + plane
 
     def present(dz, dy):
         ok = None
@@ -300,19 +300,12 @@
     def beside(dz, dy):
         return (slab + dz, plane + dy)
 
-    plane_to = [plane] + [jnp.where(plane + k < planes, plane + k, plane + k - planes) for k in range(1, planes)]
-
-    def everyone(action):
-        for to in plane_to[1:]:
-            action((slab, to))
-
-        def there(k, carry):
-            at = jnp.where(slab + k < slabs, slab + k, slab + k - slabs)
-            for to in plane_to:
-                action((at, to))
-            return carry
-
-        lax.fori_loop(1, slabs, there, 0)
+    def wrapped(at, k, count):
+        return jnp.where(at + k < count, at + k, at + k - count)
+
+    row_others = [(slab, wrapped(plane, k, planes)) for k in range(1, planes)]
+    column_others = [(wrapped(slab, k, slabs), plane) for k in range(1, slabs)]
+    corners = [(dz, dy) for dz, dy in AROUND if dz and dy]
 
     mine = [
         pltpu.make_async_copy(images.at[0], ref_ext.at[pl.ds(2, zs), pl.ds(TILE, ys)], load_sem.at[0]),
@@ -342,7 +335,16 @@
     tiles[...] = jnp.zeros(tiles.shape, F32)
     got_buf[...] = jnp.zeros(got_buf.shape, F32)
     barrier = pltpu.get_barrier_semaphore()
-    everyone(lambda to: pl.semaphore_signal(barrier, inc=1, device_id=to, device_id_type=MESH))
+
+    def greet(to):
+        pl.semaphore_signal(barrier, inc=1, device_id=to, device_id_type=MESH)
+
+    for to in row_others + column_others:
+        greet(to)
+    greeted = planes - 1 + slabs - 1
+    for dz, dy in corners:
+        pl.when(present(dz, dy))(functools.partial(greet, beside(dz, dy)))
+        greeted = greeted + jnp.where(present(dz, dy), 1, 0)
     for copy in small[:1] + mine:
         copy.wait()
     for j in range(COMPS):
@@ -352,7 +354,7 @@
         pack[side, 0:zs, :] = ref_ext[2 : 2 + zs, TILE + far, :]
         pack[side, zs : 2 * zs, :] = ref_ext[2 : 2 + zs, TILE + near, :]
         pack[side, 2 * zs :, :] = def_ext[1 : 1 + zs, TILE + near, :]
-    pl.semaphore_wait(barrier, devices - 1)
+    pl.semaphore_wait(barrier, greeted)
 
     def remote(src, dst, send, recv, to):
         return pltpu.make_async_remote_copy(
@@ -406,18 +408,28 @@
         for (dz, dy), copy in copies:
             pl.when(present(dz, dy))(copy.wait_send)
 
-    def share(stage):
-        slot = dots.at[stage, me]
-        everyone(lambda to: remote(slot, slot, dot_send.at[stage], dot_recv.at[stage], to).start())
-
-    def shared(sem, stage):
-        some = dots.at[stage, pl.ds(0, devices - 1)]
-        pltpu.make_async_copy(some, some, sem.at[stage]).wait()
+    def share(stage, row):
+        slot = row_dots.at[stage, plane]
+        row_dots[stage, plane] = jnp.broadcast_to(row, row_dots.shape[2:])
+        for to in row_others:
+            remote(slot, slot, dot_send.at[stage, 0], dot_recv.at[stage, 0], to).start()
+
+    def pass_on(stage):
+        shared(dot_recv, stage, 0)
+        slot = column_dots.at[stage, slab]
+        column_dots[stage, slab] = jnp.sum(row_dots[stage], axis=0)
+        for to in column_others:
+            remote(slot, slot, dot_send.at[stage, 1], dot_recv.at[stage, 1], to).start()
+
+    def shared(sem, stage, phase):
+        held, count = ((row_dots, planes), (column_dots, slabs))[phase]
+        if count > 1:
+            some = held.at[stage, pl.ds(0, count - 1)]
+            pltpu.make_async_copy(some, some, sem.at[stage, phase]).wait()
 
     def totals(stage):
-        shared(dot_recv, stage)
-        lanes = jnp.sum(dots[stage], axis=0)
-        return jnp.sum(lanes, axis=1, keepdims=True)
+        shared(dot_recv, stage, 1)
+        return jnp.sum(column_dots[stage], axis=0)[0:1, :]
 
     image_copies = faces()
     start_copies = around(0)
@@ -553,8 +565,6 @@
     warp(zs - 1, 0)
     for z in (0, 1, zs - 2, zs - 1):
         deep(z, 0)
-    store = pltpu.make_async_copy(model, out_model, out_sem)
-    store.start()
 
     width = across
     lines = xs // width
@@ -576,6 +586,7 @@
             w = z / elem
             g = [grads[j, z, ay, ax] for j in range(COMPS)]
             q = ref_ext[2 + z, pl.ds(pl.multiple_of(TILE + r * elem, elem), elem), ax] - model[z, ay, ax]
+            model[z, ay, ax] = q
             for ij, (i, j) in enumerate(PAIRS):
                 product = g[i] * g[j]
                 if i == j:
@@ -597,21 +608,28 @@
         return carry
 
     energy = lax.fori_loop(0, rows * lines, gather, jnp.zeros((elem, width), F32))
-    dots[0, me] = jnp.zeros(dots.shape[2:], F32)
-    dots[0, me, 0:1, :] = jnp.sum(energy, axis=0, keepdims=True)
-    share(0)
+    store = pltpu.make_async_copy(model, out_mismatch, out_sem)
+    store.start()
+    share(0, jnp.sum(energy, axis=0, keepdims=True))
     summed = dot_left(moments[...], w_stencil[...].astype(BF16))
-    load_tiles = dot_right(w_loads[...].astype(BF16), dot_left(loads[...], w_hats[...].astype(BF16)))
     send_buf[...] = dot_right(w_send[...].astype(BF16), summed)
-    for (start, used), n in zip(parts, (1, 2, 3)):
-        send_buf[start + used : start + used + TILE, :across] = load_tiles[n * TILE : (n + 1) * TILE]
     part_copies = []
     for n, ((start, used), to) in enumerate(zip(parts, ((1, 0), (0, 1), (1, 1)))):
-        at = pl.ds(start, used + TILE)
+        size = used if n == 0 else used + TILE
+        at = pl.ds(start, size)
         part_copies.append(
             (to, remote(send_buf.at[at], got_buf.at[at], part_send.at[n], part_recv.at[n], beside(*to)))
         )
-    begin(part_copies)
+    start, used = parts[0]
+    at = pl.ds(start + used, TILE)
+    part_copies.append(
+        ((1, 0), remote(send_buf.at[at], got_buf.at[at], part_send.at[3], part_recv.at[3], beside(1, 0)))
+    )
+    begin(part_copies[:1])
+    load_tiles = dot_right(w_loads[...].astype(BF16), dot_left(loads[...], w_hats[...].astype(BF16)))
+    for (start, used), n in zip(parts, (1, 2, 3)):
+        send_buf[start + used : start + used + TILE, :across] = load_tiles[n * TILE : (n + 1) * TILE]
+    begin(part_copies[1:])
     coefs[...] = dot_right(w_own[...].astype(BF16), summed)
 
     node_lane = lax.broadcasted_iota(jnp.int32, (TILE, across), 1)
@@ -638,8 +656,9 @@
     lap = lap - jnp.where(node_lane < across - 1, pltpu.roll(centre, across - 1, 1), 0.0)
     lap = jnp.where(group < COMPS, lap, 0.0)
 
-    penalty = totals(0)[0:1, :] * (reg_weight / (devices * zs * ys * xs))
+    pass_on(0)
     arrive(part_copies)
+    penalty = jnp.sum(totals(0), axis=1, keepdims=True) * (reg_weight / (devices * zs * ys * xs))
     rhs = load_tiles[0:TILE] - penalty * lap
     for start, used in parts:
         rhs = rhs + got_buf[start + used : start + used + TILE, :across]
@@ -707,13 +726,10 @@
         stacked = jnp.concatenate(lines, axis=0)
         column = jnp.sum(stacked, axis=1, keepdims=True)
         at = lax.broadcasted_iota(jnp.int32, stacked.shape, 0) == lax.broadcasted_iota(jnp.int32, stacked.shape, 1)
-        dots[stage, me] = jnp.zeros(dots.shape[2:], F32)
-        dots[stage, me, 0:1, :] = jnp.sum(jnp.where(at, column, 0.0), axis=0, keepdims=True)
-        share(stage)
+        share(stage, jnp.sum(jnp.where(at, column, 0.0), axis=0, keepdims=True))
 
     def gathered(stage, count):
-        shared(dot_recv, stage)
-        row = jnp.sum(dots[stage], axis=0)[0:1, :]
+        row = totals(stage)
         at = lax.broadcasted_iota(jnp.int32, row.shape, 1)
         return [jnp.sum(jnp.where(at == k, row, 0.0), axis=1, keepdims=True) for k in range(count)]
 
@@ -730,6 +746,7 @@
     count = 2 * BLOCK + 1
     publish(1, [basis[k // 2] * basis[(k + 1) // 2] for k in range(count)])
     listed = spread(BLOCK + 1, basis[BLOCK])
+    pass_on(1)
     landed(BLOCK + 1, listed, basis[BLOCK])
     basis.append(operate(on(BLOCK + 1), shift))
     first = gathered(1, count)
@@ -767,6 +784,7 @@
     products += [pulls[(k + 1) // 2] * chain[k // 2] for k in range(count - 1)]
     products += [chain[k // 2] * chain[(k + 1) // 2] for k in range(count - 2)]
     publish(2, products)
+    pass_on(2)
     second = gathered(2, len(products))
     seconds = (second[:count], second[count : 2 * count - 1], second[2 * count - 1 :])
     moved, _, _, _ = conjugate(([0.0], [1.0]), ([1.0], [0.0]), seconds, later, BLOCK, False)
@@ -774,11 +792,12 @@
     step = step * scale
 
     for j in range(COMPS):
-        out_step[j, 0] = step[j * rows : (j + 1) * rows]
+        out_field[j, 0] = tiles[0, j * rows : (j + 1) * rows, :] + step[j * rows : (j + 1) * rows]
     for listed in copies:
         sent(listed)
     for stage in range(3):
-        shared(dot_send, stage)
+        for phase in range(2):
+            shared(dot_send, stage, phase)
     store.wait()
 
 
@@ -798,7 +817,7 @@
     def held(*shape):
         return pltpu.VMEM(shape, F32)
 
-    step, model = pl.pallas_call(
+    return pl.pallas_call(
         functools.partial(kernel, slabs, planes, parts),
         out_shape=(
             jax.ShapeDtypeStruct(initial_displacement.shape, F32),
@@ -815,7 +834,8 @@
             held(4, zs, xs),
             held(stages, TILE, across),
             held(stages, 9, TILE, across),
-            held(3, devices, 2, across),
+            held(3, planes, 2, across),
+            held(3, slabs, 2, across),
             held(COMPS, zs, ys, xs),
             held(zs, ys, xs),
             held(COMPS * zs * ys, xs),
@@ -840,17 +860,16 @@
             dma((4,)),
             dma((stages, 8)),
             dma((stages, 8)),
-            dma((3,)),
-            dma((3,)),
-            dma((3,)),
-            dma((3,)),
+            dma((3, 2)),
+            dma((3, 2)),
+            dma((4,)),
+            dma((4,)),
         ],
         compiler_params=pltpu.CompilerParams(
             collective_id=0, has_side_effects=True, vmem_limit_bytes=56 * 1024 * 1024
         ),
         name="gauss_newton_step",
     )(images, shifts, initial_displacement, *[jnp.asarray(a) for a in arrays])
-    return initial_displacement + step, images[0] - model
 
 
 def solution(mesh):

time: 61.5 us -> 64.9 us (1.055)
  Pallas kernels: 56.8 us -> 60.9 us
  other arithmetic: 3.15 us -> 0 us
  local copies, waits for them, and re-layouts: 0.68 us -> 3.14 us
    pallas_call x1, Pallas kernels: 56.8 us -> 60.9 us  [body(): pl.pallas_call(functools.partial(kernel, slabs, planes, parts), out_shape...]
    unnamed x4, local copies, waits for them, and re-layouts: 0.68 us -> 3.14 us
    sub x1 -> x0, other arithmetic: 1.9 us -> none  [body(): return (initial_displacement + step, images[0] - model)]
    add x1 -> x0, other arithmetic: 1.25 us -> none  [body(): return (initial_displacement + step, images[0] - model)]
where the time goes in v5:
time: 64.9 us; the launch traced here: 64.7 us
  Pallas kernels  60.9 us (94%)
  local copies, waits for them, and re-layouts  3.14 us (5%)
  between operations  0.65 us (1%)
    pallas_call x1, Pallas kernels, body(): pl.pallas_call(functools.partial(kernel, slabs, planes, parts), out_shape...  60.9 us
    unnamed x4, local copies, waits for them, and re-layouts  3.14 us

profile of v5, /device:TPU:0, one launch (start us, length us, event | category | flops | bytes accessed | tf_op | source)
XLA Modules:
  0.0 64.7 jit_solution(4497947487430690904)
XLA Ops:
  0.6 60.9 %gauss_newton_step.1 = (f32[3,1,2,128]{3,2,1,0:T(2,128)}, f32[8,16,1024]{2,1,0:T(8,128)}) custom-call(f32[2,8,16,1024]{3,2,1,0:T(8,128)} %images.1, s32[3,1,2,128]{3,2,1,0:T(2,128)} %shifts_in.1, f32[3,1,2,128]{3,2,1,0:T(2,128)} %start_in.1, f32[1024,256]{1,0:T(8,128)} %constant.18.clone.w_stencil_in, f32[1024,128]{1,0:T(8,128)} %constant.19.clone.w_hats_in, ...), custom_call_target="tpu_custom_call" | custom-call | tf_op jit(solution)/shard_map/gauss_newton_step/pallas_call | solution.py:820
  61.5 0.0 copy-start
  61.6 0.7 %copy-done = f32[3,1,2,128]{3,2,1,0:T(2,128)S(1)} copy-done((f32[3,1,2,128]{3,2,1,0:T(2,128)S(1)}, f32[3,1,2,128]{3,2,1,0:T(2,128)}, u32[]{:S(2)}) %copy-start) | copy-done | bytes 3096
  62.2 0.6 copy.16
  62.8 1.9 %copy.17 = f32[8,16,1024]{2,1,0:T(8,128)} copy(f32[8,16,1024]{2,1,0:T(8,128)} %get-tuple-element.5) | data formatting | bytes 1048576
Async XLA Ops:
  61.5 0.7 %copy-start = (f32[3,1,2,128]{3,2,1,0:T(2,128)S(1)}, f32[3,1,2,128]{3,2,1,0:T(2,128)}, u32[]{:S(2)}) copy-start(f32[3,1,2,128]{3,2,1,0:T(2,128)} %get-tuple-element.4) | copy-start | bytes 9220

commit v6 on v4

--- a/solution.py
+++ b/solution.py
@@ -234,8 +234,8 @@
     w_came_in,
     w_loads_in,
     w_rise_in,
-    out_step,
-    out_model,
+    out_field,
+    out_mismatch,
     ref_ext,
     def_ext,
     def_side,
@@ -505,38 +505,47 @@
             model[z, here, :] = model[z, here, :] + gz * moved_at(0, z, r)
         return carry
 
-    def warp(z, carry):
+    def warp(z, count):
         for r in range(rows):
             here = slice(r * elem, (r + 1) * elem)
-            warped = None
+            warped = [None] * count
             for n, dx in enumerate((-1, 0, 1)):
-                s = [moves[n, j * rows + r : j * rows + r + 1, :] for j in range(2)]
-                s = [jnp.broadcast_to(v, (elem, xs)) for v in s]
-                below, above = s[0] < -0.5, s[0] > 0.5
-                line = []
-                for dy in (-1, 0, 1):
-
-                    def layer(dz):
-                        if dy == 0:
-                            return def_ext[z + 1 + dz, TILE + r * elem : TILE + (r + 1) * elem, :]
-                        return def_side[(dy + 1) // 2, z + 1 + dz, here, :]
-
-                    value = jnp.where(below, layer(-1), layer(0))
-                    line.append(jnp.where(above, layer(1), value))
-                value = jnp.where(s[1] < -0.5, line[0], line[1])
-                value = jnp.where(s[1] > 0.5, line[2], value)
-                if dx:
-                    value = along(value, dx)
-                if warped is None:
-                    warped = value
-                else:
-                    sx = jnp.broadcast_to(moves[1, 2 * rows + r : 2 * rows + r + 1, :], (elem, xs))
-                    warped = jnp.where(sx > dx - 0.5, value, warped)
-            model[z, here, :] = model[z, here, :] + warped
+                pieces = [[] for _ in range(count)]
+                for c in range(xs // across):
+                    ax = slice(c * across, (c + 1) * across)
+                    s = [moves[n, j * rows + r : j * rows + r + 1, ax] for j in range(2)]
+                    s = [jnp.broadcast_to(v, (elem, across)) for v in s]
+                    below, above = s[0] < -0.5, s[0] > 0.5
+                    left, right = s[1] < -0.5, s[1] > 0.5
+                    picked = [[] for _ in range(count)]
+                    for dy in (-1, 0, 1):
+                        layers = []
+                        for at in range(count + 2):
+                            if dy == 0:
+                                layers.append(def_ext[z + at, TILE + r * elem : TILE + (r + 1) * elem, ax])
+                            else:
+                                layers.append(def_side[(dy + 1) // 2, z + at, here, ax])
+                        for k in range(count):
+                            value = jnp.where(below, layers[k], layers[k + 1])
+                            picked[k].append(jnp.where(above, layers[k + 2], value))
+                    for k in range(count):
+                        value = jnp.where(left, picked[k][0], picked[k][1])
+                        pieces[k].append(jnp.where(right, picked[k][2], value))
+                sx = jnp.broadcast_to(moves[1, 2 * rows + r : 2 * rows + r + 1, :], (elem, xs))
+                for k in range(count):
+                    value = jnp.concatenate(pieces[k], axis=1)
+                    if dx:
+                        value = along(value, dx)
+                    warped[k] = value if n == 0 else jnp.where(sx > dx - 0.5, value, warped[k])
+            for k in range(count):
+                model[z + k, here, :] = model[z + k, here, :] + warped[k]
+
+    def warp_pair(k, carry):
+        warp(1 + 2 * k, 2)
         return carry
 
     lax.fori_loop(0, zs, flat, 0)
-    lax.fori_loop(1, zs - 1, warp, 0)
+    lax.fori_loop(0, (zs - 2) // 2, warp_pair, 0)
     lax.fori_loop(2, zs - 2, deep, 0)
     arrive(image_copies[:4] + image_copies[6:])
     clear(-1, 0, (ref_ext, (slice(0, 2),)), (def_ext, (slice(0, 1),)))
@@ -549,12 +558,10 @@
     def_ext[0, TILE - 1 : TILE, :] = got_diag[3, zs - 1 : zs, :]
     lean(0)
     lean(zs + 1)
-    warp(0, 0)
-    warp(zs - 1, 0)
+    warp(0, 1)
+    warp(zs - 1, 1)
     for z in (0, 1, zs - 2, zs - 1):
         deep(z, 0)
-    store = pltpu.make_async_copy(model, out_model, out_sem)
-    store.start()
 
     width = across
     lines = xs // width
@@ -576,6 +583,7 @@
             w = z / elem
             g = [grads[j, z, ay, ax] for j in range(COMPS)]
             q = ref_ext[2 + z, pl.ds(pl.multiple_of(TILE + r * elem, elem), elem), ax] - model[z, ay, ax]
+            model[z, ay, ax] = q
             for ij, (i, j) in enumerate(PAIRS):
                 product = g[i] * g[j]
                 if i == j:
@@ -597,21 +605,30 @@
         return carry
 
     energy = lax.fori_loop(0, rows * lines, gather, jnp.zeros((elem, width), F32))
+    store = pltpu.make_async_copy(model, out_mismatch, out_sem)
+    store.start()
     dots[0, me] = jnp.zeros(dots.shape[2:], F32)
     dots[0, me, 0:1, :] = jnp.sum(energy, axis=0, keepdims=True)
     share(0)
     summed = dot_left(moments[...], w_stencil[...].astype(BF16))
-    load_tiles = dot_right(w_loads[...].astype(BF16), dot_left(loads[...], w_hats[...].astype(BF16)))
     send_buf[...] = dot_right(w_send[...].astype(BF16), summed)
-    for (start, used), n in zip(parts, (1, 2, 3)):
-        send_buf[start + used : start + used + TILE, :across] = load_tiles[n * TILE : (n + 1) * TILE]
     part_copies = []
     for n, ((start, used), to) in enumerate(zip(parts, ((1, 0), (0, 1), (1, 1)))):
-        at = pl.ds(start, used + TILE)
+        size = used if n == 0 else used + TILE
+        at = pl.ds(start, size)
         part_copies.append(
             (to, remote(send_buf.at[at], got_buf.at[at], part_send.at[n], part_recv.at[n], beside(*to)))
         )
-    begin(part_copies)
+    start, used = parts[0]
+    at = pl.ds(start + used, TILE)
+    part_copies.append(
+        ((1, 0), remote(send_buf.at[at], got_buf.at[at], part_send.at[3], part_recv.at[3], beside(1, 0)))
+    )
+    begin(part_copies[:1])
+    load_tiles = dot_right(w_loads[...].astype(BF16), dot_left(loads[...], w_hats[...].astype(BF16)))
+    for (start, used), n in zip(parts, (1, 2, 3)):
+        send_buf[start + used : start + used + TILE, :across] = load_tiles[n * TILE : (n + 1) * TILE]
+    begin(part_copies[1:])
     coefs[...] = dot_right(w_own[...].astype(BF16), summed)
 
     node_lane = lax.broadcasted_iota(jnp.int32, (TILE, across), 1)
@@ -774,7 +791,7 @@
     step = step * scale
 
     for j in range(COMPS):
-        out_step[j, 0] = step[j * rows : (j + 1) * rows]
+        out_field[j, 0] = tiles[0, j * rows : (j + 1) * rows, :] + step[j * rows : (j + 1) * rows]
     for listed in copies:
         sent(listed)
     for stage in range(3):
@@ -798,7 +815,7 @@
     def held(*shape):
         return pltpu.VMEM(shape, F32)
 
-    step, model = pl.pallas_call(
+    return pl.pallas_call(
         functools.partial(kernel, slabs, planes, parts),
         out_shape=(
             jax.ShapeDtypeStruct(initial_displacement.shape, F32),
@@ -842,15 +859,14 @@
             dma((stages, 8)),
             dma((3,)),
             dma((3,)),
-            dma((3,)),
-            dma((3,)),
+            dma((4,)),
+            dma((4,)),
         ],
         compiler_params=pltpu.CompilerParams(
             collective_id=0, has_side_effects=True, vmem_limit_bytes=56 * 1024 * 1024
         ),
         name="gauss_newton_step",
     )(images, shifts, initial_displacement, *[jnp.asarray(a) for a in arrays])
-    return initial_displacement + step, images[0] - model
 
 
 def solution(mesh):

time: 61.5 us -> 60.9 us (level)
  other arithmetic: 3.15 us -> 0 us
  local copies, waits for them, and re-layouts: 0.68 us -> 3.14 us
    unnamed x4, local copies, waits for them, and re-layouts: 0.68 us -> 3.14 us
    sub x1 -> x0, other arithmetic: 1.9 us -> none  [body(): return (initial_displacement + step, images[0] - model)]
    add x1 -> x0, other arithmetic: 1.25 us -> none  [body(): return (initial_displacement + step, images[0] - model)]
where the time goes in v6:
time: 60.9 us; the launch traced here: 60.8 us
  Pallas kernels  57 us (94%)
  local copies, waits for them, and re-layouts  3.14 us (5%)
  between operations  0.65 us (1%)
    pallas_call x1, Pallas kernels, body(): pl.pallas_call(functools.partial(kernel, slabs, planes, parts), out_shape...  57 us
    unnamed x4, local copies, waits for them, and re-layouts  3.14 us

profile of v6, /device:TPU:0, one launch (start us, length us, event | category | flops | bytes accessed | tf_op | source)
XLA Modules:
  0.0 60.8 jit_solution(8453842597420819512)
XLA Ops:
  0.6 57.0 %gauss_newton_step.1 = (f32[3,1,2,128]{3,2,1,0:T(2,128)}, f32[8,16,1024]{2,1,0:T(8,128)}) custom-call(f32[2,8,16,1024]{3,2,1,0:T(8,128)} %images.1, s32[3,1,2,128]{3,2,1,0:T(2,128)} %shifts_in.1, f32[3,1,2,128]{3,2,1,0:T(2,128)} %start_in.1, f32[1024,256]{1,0:T(8,128)} %constant.18.clone.w_stencil_in, f32[1024,128]{1,0:T(8,128)} %constant.19.clone.w_hats_in, ...), custom_call_target="tpu_custom_call" | custom-call | tf_op jit(solution)/shard_map/gauss_newton_step/pallas_call | solution.py:818
  57.6 0.0 copy-start
  57.6 0.7 %copy-done = f32[3,1,2,128]{3,2,1,0:T(2,128)S(1)} copy-done((f32[3,1,2,128]{3,2,1,0:T(2,128)S(1)}, f32[3,1,2,128]{3,2,1,0:T(2,128)}, u32[]{:S(2)}) %copy-start) | copy-done | bytes 3096
  58.3 0.6 copy.16
  58.9 1.9 %copy.17 = f32[8,16,1024]{2,1,0:T(8,128)} copy(f32[8,16,1024]{2,1,0:T(8,128)} %get-tuple-element.5) | data formatting | bytes 1048576
Async XLA Ops:
  57.6 0.7 %copy-start = (f32[3,1,2,128]{3,2,1,0:T(2,128)S(1)}, f32[3,1,2,128]{3,2,1,0:T(2,128)}, u32[]{:S(2)}) copy-start(f32[3,1,2,128]{3,2,1,0:T(2,128)} %get-tuple-element.4) | copy-start | bytes 9220
